TPU v7x, 512 devices: a whole 4x4x16 slice. The times are simulated.
512 devices in a mesh: row: 16 (over z_lo, y), col: 4 (over z_hi), rep: 8 (over x, core).
Axes of the slice: x: 4, y: 4, z: 16 (z_hi: 4, z_lo: 4; z = z_hi * 4 + z_lo), core: 2. Of those that a mesh axis runs over, the one named last changes fastest.
Arguments:
- x_t: bfloat16 [128, 65536], P('rep', ('row', 'col')), may hold values from -6 to 6
- weight: bfloat16 [128, 256], replicated, may hold values from -0.5 to 0.5
- cotangent_t: bfloat16 [256, 65536], P('rep', ('row', 'col')), may hold values from -6 to 6
- tile_vals: bfloat16 [16, 4, 96, 128, 128], P('row', 'col'), may hold values from -0.625 to 0.625
- tile_rows: int32 [16, 4, 96], P('row', 'col'), may hold values from 0 to 31, as said below
- tile_cols: int32 [16, 4, 96], P('row', 'col'), may hold values from 0 to 127
- tile_count: int32 [16, 4], P('row', 'col'), may hold values from 1 to 96, as said below
Outputs:
- y_t: bfloat16 [256, 65536], P('rep', ('row', 'col'))
- dx_t: float32 [128, 65536], P('rep', ('row', 'col'))
- weight_grad: float32 [128, 256], P(None, 'rep')
Inputs may be any that keep to these rules, and one draw needn't show every extreme that they name: Together with tile_cols at the same index, tile_rows gives within one grid block 96 distinct (row tile, column tile) pairs; entries at t >= tile_count are not part of the graph. `tile_count`: some grid block lists exactly 96 live tiles in every draw.
All inputs are finite; a program needn't handle non-finite values.
Results may differ from a plain program's by a relative error of at most 0.0054.
Values may be sent and summed in bfloat16 or wider, within the bound.
No kernel may reach another device: no remote copies, remote signals or barrier semaphores. Data moves between devices by JAX's collectives and lax.ppermute only.
A program may use at most 64 MiB of HBM per device.

v0:
```python
import jax
import jax.numpy as jnp
from jax import lax
from jax.sharding import PartitionSpec as P


def local(x_t, weight, cotangent_t, tile_vals, tile_rows, tile_cols, tile_count):
    feat_loc = x_t.shape[0]
    slab = x_t.shape[1]
    tile = tile_vals.shape[-1]
    values = tile_vals[0, 0]
    rows = tile_rows[0, 0]
    cols = tile_cols[0, 0]
    listed = values.shape[0]
    live = lax.iota(jnp.int32, listed) < tile_count[0, 0]
    row_tiles = lax.axis_size("col") * (slab // tile)
    col_tiles = lax.axis_size("row") * (slab // tile)
    row_onehot = (
        (rows[:, None] == lax.iota(jnp.int32, row_tiles)[None, :]) & live[:, None]
    ).astype(jnp.float32)
    col_onehot = (
        (cols[:, None] == lax.iota(jnp.int32, col_tiles)[None, :]) & live[:, None]
    ).astype(jnp.float32)
    column_block = lax.all_gather(x_t, "row", axis=1, tiled=True).reshape(feat_loc, col_tiles, tile)
    picked = jnp.take(column_block, cols, axis=1)
    product = jnp.einsum("ftk,tnk->ftn", picked, values, preferred_element_type=jnp.float32)
    partial_value = jnp.einsum("ftn,tr->frn", product, row_onehot, precision=lax.Precision.HIGHEST)
    partial_value = partial_value.reshape(feat_loc, row_tiles * tile)
    hidden_mine = lax.psum_scatter(partial_value, "col", scatter_dimension=1, tiled=True).astype(
        jnp.bfloat16
    )
    hidden_all = lax.all_gather(hidden_mine, "rep", axis=0, tiled=True)
    rep_at = lax.axis_index("rep")
    out_loc = weight.shape[1] // lax.axis_size("rep")
    w_cols = lax.dynamic_slice_in_dim(weight, rep_at * out_loc, out_loc, 1)
    pre_mine = jnp.dot(w_cols.T, hidden_all, preferred_element_type=jnp.float32)
    y_mine = jax.nn.silu(pre_mine).astype(jnp.bfloat16)
    sig = jax.nn.sigmoid(pre_mine)
    dpre = (cotangent_t.astype(jnp.float32) * sig * (1.0 + pre_mine * (1.0 - sig))).astype(
        jnp.bfloat16
    )
    grad_part = jnp.dot(hidden_all, dpre.T, preferred_element_type=jnp.float32)
    weight_grad = lax.psum(grad_part, ("row", "col"))
    grad_terms = jnp.dot(w_cols, dpre, preferred_element_type=jnp.float32)
    dagg_mine = lax.psum_scatter(grad_terms, "rep", scatter_dimension=0, tiled=True).astype(
        jnp.bfloat16
    )
    row_block = lax.all_gather(dagg_mine, "col", axis=1, tiled=True).reshape(
        feat_loc, row_tiles, tile
    )
    grad_picked = jnp.take(row_block, rows, axis=1)
    backward = jnp.einsum("ftn,tnk->ftk", grad_picked, values, preferred_element_type=jnp.float32)
    column_sum = jnp.einsum("ftk,tc->fck", backward, col_onehot, precision=lax.Precision.HIGHEST)
    column_sum = column_sum.reshape(feat_loc, col_tiles * tile)
    dx_mine = lax.psum_scatter(column_sum, "row", scatter_dimension=1, tiled=True)
    return (y_mine, dx_mine, weight_grad)


def solution(mesh):
    return jax.shard_map(
        local,
        mesh=mesh,
        in_specs=(
            P("rep", ("row", "col")),
            P(),
            P("rep", ("row", "col")),
            P("row", "col", None, None, None),
            P("row", "col", None),
            P("row", "col", None),
            P("row", "col"),
        ),
        out_specs=(P("rep", ("row", "col")), P("rep", ("row", "col")), P(None, "rep")),
        check_vma=False,
    )
```

profile of v0, /device:TPU:32, one launch (start us, length us, event | category | flops | bytes accessed | tf_op | source)
XLA Modules:
  0.0 578.8 jit_solution(9639889617259612786)
XLA Ops:
  7.2 0.8 compare_and_fusion.1
  8.0 0.7 fusion.36
  9.5 39.2 %all_gather.9 = bf16[16,16384]{1,0:T(8,128)(2,1)S(1)} all-gather(bf16[16,1024]{1,0:T(8,128)(2,1)} %param.7), channel_id=1, replica_groups=mesh['row'=16,'col'=4,'rep'=8] {'row'}, dimensions={1}, use_global_device_ids=true | all-gather | bytes 557056 | tf_op jit(solution)/shard_map/all_gather | solution.py:24
  48.7 0.9 copy_bitcast_fusion.1
  49.6 1.7 gather_fusion
  51.3 1.8 fusion.4
  53.1 0.6 fusion.12
  53.7 0.8 copy.28
  54.6 42.6 %reduce-scatter.4.cloned.1.call-done = f32[16,1024]{1,0:T(8,128)} async-done(((f32[16,4096]{1,0:T(8,128)}), f32[16,1024]{1,0:T(8,128)}) %reduce-scatter.4.cloned.1.call-update) | async-done | bytes 65552 | tf_op jit(solution)/shard_map/reduce_scatter | solution.py:29
  97.2 0.8 convert_element_type.17
  98.0 12.8 %all_gather.10 = bf16[128,1024]{1,0:T(8,128)(2,1)S(1)} all-gather(bf16[16,1024]{1,0:T(8,128)(2,1)S(1)} %convert_element_type.17), channel_id=1, replica_groups=mesh['row'=16,'col'=4,'rep'=8] {'rep'}, dimensions={0}, use_global_device_ids=true | all-gather | bytes 294912 | tf_op jit(solution)/shard_map/all_gather | solution.py:32
  110.9 1.8 multiply_convert_fusion
  112.7 0.6 copy-done.1
  113.3 1.1 fusion.25
  114.5 0.5 compare_and_fusion
  115.0 34.7 %reduce-scatter.6.cloned.1.call-done = f32[16,1024]{1,0:T(8,128)} async-done(((f32[128,1024]{1,0:T(8,128)}), f32[16,1024]{1,0:T(8,128)}) %reduce-scatter.6.cloned.1.call-update) | async-done | bytes 65552 | tf_op jit(solution)/shard_map/reduce_scatter | solution.py:45
  149.7 0.8 convert_element_type.21
  150.6 22.4 %all_gather.11 = bf16[16,4096]{1,0:T(8,128)(2,1)S(1)} all-gather(bf16[16,1024]{1,0:T(8,128)(2,1)S(1)} %convert_element_type.21), channel_id=1, replica_groups=mesh['row'=16,'col'=4,'rep'=8] {'col'}, dimensions={1}, use_global_device_ids=true | all-gather | bytes 163840 | tf_op jit(solution)/shard_map/all_gather | solution.py:48
  172.9 1.4 gather_fusion.1
  174.3 2.0 fusion.7
  176.3 0.9 fusion.10
  177.2 1.6 copy.27
  178.9 0.2 fusion.42
  179.0 393.3 %psum.7 = f32[128,32]{0,1:T(8,128)} all-reduce(f32[128,32]{0,1:T(8,128)S(1)} %fusion.42), channel_id=1, replica_groups=mesh['row'=16,'col'=4,'rep'=8] {'row','col'}, use_global_device_ids=true, to_apply=%region_3.4 | all-reduce | flops 4096 | bytes 32768 | tf_op jit(solution)/shard_map/psum | solution.py:43
  (23 shorter events, 0.2 us)
Async XLA Ops:
  7.2 44.1 %copy-start = (bf16[1,1,96,128,128]{4,3,2,1,0:T(8,128)(2,1)S(1)}, bf16[1,1,96,128,128]{4,3,2,1,0:T(8,128)(2,1)}, u32[]{:S(2)}) copy-start(bf16[1,1,96,128,128]{4,3,2,1,0:T(8,128)(2,1)} %param.10) | copy-start | bytes 9437188
  7.2 90.0 %reduce-scatter.4.cloned.1.call-start = ((), (), s32[]{:S(2)}) async-start(), calls=%async_computation.3 | async-start | bytes 327680 | tf_op jit(solution)/shard_map/reduce_scatter | solution.py:29
  48.7 4.4 copy-start.4
  53.1 60.2 %copy-start.3 = (bf16[128,256]{1,0:T(8,128)(2,1)S(1)}, bf16[128,256]{1,0:T(8,128)(2,1)}, u32[]{:S(2)}) copy-start(bf16[128,256]{1,0:T(8,128)(2,1)} %param.8) | copy-start | bytes 196612
  54.6 95.1 %reduce-scatter.6.cloned.1.call-start = ((), (), s32[]{:S(2)}) async-start(), calls=%async_computation.4 | async-start | bytes 589824 | tf_op jit(solution)/shard_map/reduce_scatter | solution.py:45
  112.7 0.6 copy-start.1
  114.4 62.0 %copy-start.5 = (s32[1,1,96]{2,1,0:T(1,128)S(1)}, s32[1,1,96]{2,1,0:T(1,128)}, u32[]{:S(2)}) copy-start(s32[1,1,96]{2,1,0:T(1,128)} %param.12) | copy-start | bytes 1156
  114.4 457.9 %reduce-scatter.8.cloned.1.call-start = ((), (), s32[]{:S(2)}) async-start(), calls=%async_computation.5 | async-start | bytes 1114112 | tf_op jit(solution)/shard_map/reduce_scatter | solution.py:55
  176.3 2.5 copy-start.2
Sparse Core Ops, SparseCore 0:
  54.7 42.4 reduce-scatter.3
  114.5 35.1 reduce-scatter.5
  179.0 78.3 reduce-scatter.7
where the time goes:
time: 579 us
  blocking collectives  468 us (81%)
  waiting for transfers between devices  77.4 us (13%)
  between operations  14.5 us (3%)
  matrix products  8.31 us (1%)
  local copies, waits for them, and re-layouts  7.09 us (1%)
    psum x1, blocking collectives, local(): weight_grad = lax.psum(grad_part, ('row', 'col'))  393 us
    reduce_scatter x1, waiting for transfers between devices, local(): lax.psum_scatter(partial_value, 'col', scatter_dimension=1, tiled=True)  42.6 us
    all_gather x1, blocking collectives, local(): lax.all_gather(x_t, 'row', axis=1, tiled=True)  39.2 us
    reduce_scatter x1, waiting for transfers between devices, local(): lax.psum_scatter(grad_terms, 'rep', scatter_dimension=0, tiled=True)  34.7 us
    all_gather x1, blocking collectives, local(): lax.all_gather(dagg_mine, 'col', axis=1, tiled=True)  22.4 us
    all_gather x1, blocking collectives, local(): hidden_all = lax.all_gather(hidden_mine, 'rep', axis=0, tiled=True)  12.8 us
  transfers between devices with their start and end apart: 3, of which 2 were waited for; matrix products, arithmetic and copies ran while one was open for 0% of the time, Pallas kernels for 0%

commit v1 on v0

v1 whole, which is shorter than its diff:
```python
import functools

import jax
import jax.numpy as jnp
from jax import lax
from jax.experimental import pallas as pl
from jax.experimental.pallas import tpu as pltpu
from jax.sharding import PartitionSpec as P

BF16 = jnp.bfloat16
F32 = jnp.float32
UNROLL = 8
SMEM = pl.BlockSpec(memory_space=pltpu.SMEM)
VMEM = pl.BlockSpec(memory_space=pltpu.VMEM)
PARAMS = pltpu.CompilerParams(vmem_limit_bytes=32 * 1024 * 1024)


def live_loop(count, body):
    groups = count // UNROLL

    def group(g, carry):
        body(g * UNROLL, UNROLL)
        return carry

    def single(t, carry):
        body(t, 1)
        return carry

    lax.fori_loop(0, groups, group, 0)
    lax.fori_loop(groups * UNROLL, count, single, 0)


def aggregate_kernel(rows, cols, count, x_ref, vals_ref, out_ref, acc):
    acc[...] = jnp.zeros_like(acc)

    def body(first, n):
        products = [
            lax.dot_general(
                x_ref[cols[first + u]],
                vals_ref[first + u],
                (((1,), (1,)), ((), ())),
                preferred_element_type=F32,
            )
            for u in range(n)
        ]
        for u in range(n):
            at = rows[first + u]
            acc[at] = acc[at] + products[u]

    live_loop(count[0], body)
    out_ref[...] = acc[...].astype(out_ref.dtype)


def middle_kernel(h_ref, wt_ref, w_ref, cot_ref, y_ref, terms_ref, grad_ref):
    groups, tiles, feat, tile = h_ref.shape
    wt = wt_ref[...]
    w = w_ref[...]
    grad = jnp.zeros(grad_ref.shape, F32)
    for i in range(tiles):
        at = slice(i * tile, (i + 1) * tile)
        h = h_ref[:, i].reshape(groups * feat, tile)
        pre = jnp.dot(wt, h, preferred_element_type=F32)
        sig = jax.nn.sigmoid(pre)
        y_ref[:, at] = (pre * sig).astype(y_ref.dtype)
        dpre = (cot_ref[:, at].astype(F32) * sig * (1.0 + pre * (1.0 - sig))).astype(BF16)
        terms = jnp.dot(w, dpre, preferred_element_type=F32)
        terms_ref[:, i] = terms.astype(terms_ref.dtype).reshape(groups, feat, tile)
        grad += lax.dot_general(
            dpre, h, (((1,), (1,)), ((), ())), preferred_element_type=F32
        )
    grad_ref[...] = grad


def backward_kernel(rows, cols, count, d_ref, vals_ref, out_ref, acc):
    row_parts, _, tile = out_ref.shape
    feat = acc.shape[1]
    per = acc.shape[0] // row_parts
    slab_rows = per * feat
    acc[...] = jnp.zeros_like(acc)

    def body(first, n):
        products = []
        for u in range(n):
            at = rows[first + u]
            start = pl.multiple_of((at % per) * feat, feat)
            products.append(
                jnp.dot(
                    d_ref[at // per, pl.ds(start, feat), :],
                    vals_ref[first + u],
                    preferred_element_type=F32,
                )
            )
        for u in range(n):
            at = cols[first + u]
            acc[at] = acc[at] + products[u]

    live_loop(count[0], body)
    grad = jnp.sum(d_ref[:, slab_rows:, :].astype(F32), axis=0).astype(out_ref.dtype)
    for r in range(row_parts):
        out_ref[r, :slab_rows, :] = (
            acc[r * per : (r + 1) * per].reshape(slab_rows, tile).astype(out_ref.dtype)
        )
        out_ref[r, slab_rows:, :] = grad


def final_kernel(in_ref, dx_ref, grad_ref):
    feat = dx_ref.shape[0]
    tile = in_ref.shape[2]
    slab_rows = in_ref.shape[1] - grad_ref.shape[0]
    for i in range(slab_rows // feat):
        dx_ref[:, i * tile : (i + 1) * tile] = jnp.sum(
            in_ref[:, i * feat : (i + 1) * feat, :].astype(F32), axis=0
        )
    grad_ref[...] = jnp.sum(in_ref[:, slab_rows:, :].astype(F32), axis=0)


def exchange(parts, axis):
    return lax.all_to_all(parts, axis, 0, 0, tiled=True)


def local(x_t, weight, cotangent_t, tile_vals, tile_rows, tile_cols, tile_count):
    feat, slab = x_t.shape
    tile = tile_vals.shape[-1]
    per = slab // tile
    n_row, n_col, n_rep = lax.axis_size("row"), lax.axis_size("col"), lax.axis_size("rep")
    values = tile_vals[0, 0]
    rows = tile_rows[0, 0]
    cols = tile_cols[0, 0]
    count = tile_count[0]
    out_loc = weight.shape[1] // n_rep
    w_cols = lax.dynamic_slice_in_dim(weight, lax.axis_index("rep") * out_loc, out_loc, 1)

    x_tiles = x_t.reshape(feat, per, tile).transpose(1, 0, 2)
    x_all = exchange(jnp.broadcast_to(x_tiles[None], (n_row, per, feat, tile)), "row")

    part = pl.pallas_call(
        aggregate_kernel,
        out_shape=jax.ShapeDtypeStruct((n_col * per, feat, tile), BF16),
        in_specs=[SMEM, SMEM, SMEM, VMEM, VMEM],
        out_specs=VMEM,
        scratch_shapes=[pltpu.VMEM((n_col * per, feat, tile), F32)],
        compiler_params=PARAMS,
        name="aggregate",
    )(rows, cols, count, x_all.reshape(n_row * per, feat, tile), values)

    part = exchange(part.reshape(n_col, per, feat, tile), "col")
    mine = jnp.sum(part.astype(F32), axis=0).astype(BF16)
    h_all = exchange(jnp.broadcast_to(mine[None], (n_rep, per, feat, tile)), "rep")

    y, terms, grad = pl.pallas_call(
        middle_kernel,
        out_shape=(
            jax.ShapeDtypeStruct((out_loc, slab), BF16),
            jax.ShapeDtypeStruct((n_rep, per, feat, tile), BF16),
            jax.ShapeDtypeStruct((out_loc, n_rep * feat), F32),
        ),
        in_specs=[VMEM] * 4,
        out_specs=(VMEM, VMEM, VMEM),
        compiler_params=PARAMS,
        name="middle",
    )(h_all, w_cols.T, w_cols, cotangent_t)

    terms = exchange(terms, "rep")
    dagg = jnp.sum(terms.astype(F32), axis=0).astype(BF16)
    grad_rows = out_loc * n_rep * feat // tile
    send = jnp.concatenate(
        [dagg.reshape(per * feat, tile), grad.reshape(grad_rows, tile).astype(BF16)], axis=0
    )
    d_all = exchange(jnp.broadcast_to(send[None], (n_col,) + send.shape), "col")

    back = pl.pallas_call(
        backward_kernel,
        out_shape=jax.ShapeDtypeStruct((n_row,) + send.shape, BF16),
        in_specs=[SMEM, SMEM, SMEM, VMEM, VMEM],
        out_specs=VMEM,
        scratch_shapes=[pltpu.VMEM((n_row * per, feat, tile), F32)],
        compiler_params=PARAMS,
        name="backward",
    )(rows, cols, count, d_all, values)
    back = exchange(back, "row")

    dx, grad = pl.pallas_call(
        final_kernel,
        out_shape=(
            jax.ShapeDtypeStruct((feat, slab), F32),
            jax.ShapeDtypeStruct((grad_rows, tile), F32),
        ),
        in_specs=[VMEM],
        out_specs=(VMEM, VMEM),
        compiler_params=PARAMS,
        name="final",
    )(back)
    return y, dx, grad.reshape(out_loc, n_rep * feat).T


def solution(mesh):
    return jax.shard_map(
        local,
        mesh=mesh,
        in_specs=(
            P("rep", ("row", "col")),
            P(),
            P("rep", ("row", "col")),
            P("row", "col", None, None, None),
            P("row", "col", None),
            P("row", "col", None),
            P("row", "col"),
        ),
        out_specs=(P("rep", ("row", "col")), P("rep", ("row", "col")), P(None, "rep")),
        check_vma=False,
    )
```

time: 579 us -> 129 us (0.22)
  the two profiles are of different devices: /device:TPU:32 before, /device:TPU:1 now
where the time goes in v1:
time: 129 us; the launch traced here: 128 us
  blocking collectives  64.4 us (50%)
  waiting for transfers between devices  25.7 us (20%)
  starting transfers between devices  21.3 us (17%)
  local copies, waits for them, and re-layouts  9.3 us (7%)
  Pallas kernels  6.12 us (5%)
  between operations  1.37 us (1%)
    all_to_all x3, blocking collectives, exchange(): return lax.all_to_all(parts, axis, 0, 0, tiled=True)  64.4 us
    all_to_all x3, waiting for transfers between devices, exchange(): return lax.all_to_all(parts, axis, 0, 0, tiled=True)  25.7 us
    all_to_all x3, starting transfers between devices, exchange(): return lax.all_to_all(parts, axis, 0, 0, tiled=True)  21.3 us
    unnamed x23, local copies, waits for them, and re-layouts  7.39 us
  transfers between devices with their start and end apart: 3, of which 3 were waited for; matrix products, arithmetic and copies ran while one was open for 0% of the time, Pallas kernels for 0%

profile of v1, /device:TPU:1, one launch (start us, length us, event | category | flops | bytes accessed | tf_op | source)
XLA Modules:
  0.0 128.3 jit_solution(4625032344690279249)
XLA Ops:
  0.6 0.8 copy.12
  1.5 0.9 broadcast_in_dim.6
  2.4 9.2 %all-to-all-start = ((bf16[16,8,16,128]{3,2,1,0:T(8,128)(2,1)}), bf16[16,8,16,128]{3,2,1,0:T(8,128)(2,1)S(1)}, u32[]{:S(2)}, u32[]{:S(2)}) async-start(bf16[16,8,16,128]{3,2,1,0:T(8,128)(2,1)} %broadcast_in_dim.6), calls=%async_computation | async-start | bytes 1048576 | tf_op jit(solution)/shard_map/all_to_all | solution.py:118
  12.2 13.0 %all-to-all-done = bf16[16,8,16,128]{3,2,1,0:T(8,128)(2,1)S(1)} async-done(((bf16[16,8,16,128]{3,2,1,0:T(8,128)(2,1)}), bf16[16,8,16,128]{3,2,1,0:T(8,128)(2,1)S(1)}, u32[]{:S(2)}, u32[]{:S(2)}) %all-to-all-start) | async-done | bytes 524320 | tf_op jit(solution)/shard_map/all_to_all | solution.py:118
  25.2 0.8 copy-done.3
  26.0 1.9 %copy-done.1 = bf16[1,1,96,128,128]{4,3,2,1,0:T(8,128)(2,1)S(1)} copy-done((bf16[1,1,96,128,128]{4,3,2,1,0:T(8,128)(2,1)S(1)}, bf16[1,1,96,128,128]{4,3,2,1,0:T(8,128)(2,1)}, u32[]{:S(2)}) %copy-start.1) | copy-done | bytes 3145752
  27.9 1.0 copy-done.4
  28.9 0.7 copy-done.7
  29.6 0.7 copy-done.9
  30.2 1.8 %aggregate.1 = bf16[32,16,128]{2,1,0:T(8,128)(2,1)S(1)} custom-call(s32[96]{0:T(128)S(1)} %bitcast.20, s32[96]{0:T(128)S(1)} %bitcast.22, s32[1]{0:T(128)} %bitcast.14.count, bf16[128,16,128]{2,1,0:T(8,128)(2,1)S(1)} %bitcast.18, bf16[96,128,128]{2,1,0:T(8,128)(2,1)S(1)} %bitcast.16), custom_call_target="tpu_custom_call" | custom-call | tf_op jit(solution)/shard_map/aggregate/pallas_call | solution.py:136
  32.1 25.7 %all_to_all.30 = bf16[4,8,16,128]{3,2,1,0:T(8,128)(2,1)S(1)} all-to-all(bf16[4,8,16,128]{3,2,1,0:T(8,128)(2,1)S(1)} %bitcast.19), channel_id=1, replica_groups=mesh['row'=16,'col'=4,'rep'=8] {'col'}, dimensions={0} | all-to-all | bytes 262144 | tf_op jit(solution)/shard_map/all_to_all | solution.py:118
  57.8 0.7 broadcast_in_dim.7
  58.5 7.8 %all-to-all-start.2 = ((bf16[8,8,16,128]{3,2,1,0:T(8,128)(2,1)}), bf16[8,8,16,128]{3,2,1,0:T(8,128)(2,1)S(1)}, u32[]{:S(2)}, u32[]{:S(2)}) async-start(bf16[8,8,16,128]{3,2,1,0:T(8,128)(2,1)} %broadcast_in_dim.7), calls=%async_computation.2 | async-start | bytes 524288 | tf_op jit(solution)/shard_map/all_to_all | solution.py:118
  66.4 0.1 constant_dynamic-slice_fusion.w_ref
  66.5 6.2 %all-to-all-done.2.h_ref = bf16[8,8,16,128]{3,2,1,0:T(8,128)(2,1)S(1)} async-done(((bf16[8,8,16,128]{3,2,1,0:T(8,128)(2,1)}), bf16[8,8,16,128]{3,2,1,0:T(8,128)(2,1)S(1)}, u32[]{:S(2)}, u32[]{:S(2)}) %all-to-all-start.2) | async-done | bytes 262176 | tf_op jit(solution)/shard_map/all_to_all | solution.py:118
  72.8 0.8 copy-done.6
  73.6 1.9 %middle.1 = (bf16[32,1024]{1,0:T(8,128)(2,1)}, bf16[8,8,16,128]{3,2,1,0:T(8,128)(2,1)S(1)}, f32[32,128]{1,0:T(8,128)S(1)}) custom-call(bf16[8,8,16,128]{3,2,1,0:T(8,128)(2,1)S(1)} %all-to-all-done.2.h_ref, bf16[32,128]{1,0:T(8,128)(2,1)S(1)} %copy.11.wt_ref, bf16[128,32]{1,0:T(8,128)(2,1)S(1)} %constant_dynamic-slice_fusion.w_ref, bf16[32,1024]{1,0:T(8,128)(2,1)S(1)} %copy-done.6), custom_call_target="tpu_custom_call" | custom-call | tf_op jit(solution)/shard_map/middle/pallas_call | solution.py:150
  75.5 0.7 copy-done.5
  76.2 4.4 %all-to-all-start.3 = ((bf16[8,8,16,128]{3,2,1,0:T(8,128)(2,1)}), bf16[8,8,16,128]{3,2,1,0:T(8,128)(2,1)S(1)}, u32[]{:S(2)}, u32[]{:S(2)}) async-start(bf16[8,8,16,128]{3,2,1,0:T(8,128)(2,1)} %copy-done.5), calls=%async_computation.3 | async-start | bytes 524288 | tf_op jit(solution)/shard_map/all_to_all | solution.py:118
  80.5 6.5 %all-to-all-done.3 = bf16[8,8,16,128]{3,2,1,0:T(8,128)(2,1)S(1)} async-done(((bf16[8,8,16,128]{3,2,1,0:T(8,128)(2,1)}), bf16[8,8,16,128]{3,2,1,0:T(8,128)(2,1)S(1)}, u32[]{:S(2)}, u32[]{:S(2)}) %all-to-all-start.3) | async-done | bytes 262176 | tf_op jit(solution)/shard_map/all_to_all | solution.py:118
  87.1 15.3 %all_to_all.31.d_ref = bf16[4,160,128]{2,1,0:T(8,128)(2,1)S(1)} all-to-all(bf16[4,160,128]{2,1,0:T(8,128)(2,1)S(1)} %broadcast_in_dim.8), channel_id=1, replica_groups=mesh['row'=16,'col'=4,'rep'=8] {'col'}, dimensions={0} | all-to-all | bytes 327680 | tf_op jit(solution)/shard_map/all_to_all | solution.py:118
  102.5 1.7 %backward.1 = bf16[16,160,128]{2,1,0:T(8,128)(2,1)S(1)} custom-call(s32[96]{0:T(128)S(1)} %bitcast.21, s32[96]{0:T(128)S(1)} %bitcast.23, s32[1]{0:T(128)} %bitcast.15.count, bf16[4,160,128]{2,1,0:T(8,128)(2,1)S(1)} %all_to_all.31.d_ref, bf16[96,128,128]{2,1,0:T(8,128)(2,1)S(1)} %bitcast.17), custom_call_target="tpu_custom_call" | custom-call | tf_op jit(solution)/shard_map/backward/pallas_call | solution.py:171
  104.2 23.4 %all_to_all.32.in_ref = bf16[16,160,128]{2,1,0:T(8,128)(2,1)S(1)} all-to-all(bf16[16,160,128]{2,1,0:T(8,128)(2,1)S(1)} %backward.1), channel_id=1, replica_groups=mesh['row'=16,'col'=4,'rep'=8] {'row'}, dimensions={0} | all-to-all | bytes 1310720 | tf_op jit(solution)/shard_map/all_to_all | solution.py:118
  127.6 0.7 final.1
  (23 shorter events, 0.3 us)
Async XLA Ops:
  0.6 65.6 %copy-start = (bf16[128,256]{1,0:T(8,128)(2,1)S(1)}, bf16[128,256]{1,0:T(8,128)(2,1)}, u32[]{:S(2)}) copy-start(bf16[128,256]{1,0:T(8,128)(2,1)} %param.8) | copy-start | bytes 196612
  2.4 22.8 %all-to-all-start = ((bf16[16,8,16,128]{3,2,1,0:T(8,128)(2,1)}), bf16[16,8,16,128]{3,2,1,0:T(8,128)(2,1)S(1)}, u32[]{:S(2)}, u32[]{:S(2)}) async-start(bf16[16,8,16,128]{3,2,1,0:T(8,128)(2,1)} %broadcast_in_dim.6), calls=%async_computation | async-start | bytes 1048576 | tf_op jit(solution)/shard_map/all_to_all | solution.py:118
  25.2 0.8 copy-start.3
  26.0 1.9 %copy-start.1 = (bf16[1,1,96,128,128]{4,3,2,1,0:T(8,128)(2,1)S(1)}, bf16[1,1,96,128,128]{4,3,2,1,0:T(8,128)(2,1)}, u32[]{:S(2)}) copy-start(bf16[1,1,96,128,128]{4,3,2,1,0:T(8,128)(2,1)} %param.10) | copy-start | bytes 9437188
  27.9 1.0 copy-start.4
  28.9 0.7 copy-start.7
  29.6 0.7 copy-start.9
  30.2 72.2 %copy-start.2 = (bf16[1,1,96,128,128]{4,3,2,1,0:T(8,128)(2,1)S(1)}, bf16[1,1,96,128,128]{4,3,2,1,0:T(8,128)(2,1)}, u32[]{:S(2)}) copy-start(bf16[1,1,96,128,128]{4,3,2,1,0:T(8,128)(2,1)} %param.10) | copy-start | bytes 9437188
  30.2 72.2 %copy-start.8 = (s32[1,1,96]{2,1,0:T(1,128)S(1)}, s32[1,1,96]{2,1,0:T(1,128)}, u32[]{:S(2)}) copy-start(s32[1,1,96]{2,1,0:T(1,128)} %param.11) | copy-start | bytes 1156
  30.2 72.2 %copy-start.10 = (s32[1,1,96]{2,1,0:T(1,128)S(1)}, s32[1,1,96]{2,1,0:T(1,128)}, u32[]{:S(2)}) copy-start(s32[1,1,96]{2,1,0:T(1,128)} %param.12) | copy-start | bytes 1156
  58.5 14.3 %all-to-all-start.2 = ((bf16[8,8,16,128]{3,2,1,0:T(8,128)(2,1)}), bf16[8,8,16,128]{3,2,1,0:T(8,128)(2,1)S(1)}, u32[]{:S(2)}, u32[]{:S(2)}) async-start(bf16[8,8,16,128]{3,2,1,0:T(8,128)(2,1)} %broadcast_in_dim.7), calls=%async_computation.2 | async-start | bytes 524288 | tf_op jit(solution)/shard_map/all_to_all | solution.py:118
  72.8 0.8 copy-start.6
  75.5 0.7 copy-start.5
  76.2 10.9 %all-to-all-start.3 = ((bf16[8,8,16,128]{3,2,1,0:T(8,128)(2,1)}), bf16[8,8,16,128]{3,2,1,0:T(8,128)(2,1)S(1)}, u32[]{:S(2)}, u32[]{:S(2)}) async-start(bf16[8,8,16,128]{3,2,1,0:T(8,128)(2,1)} %copy-done.5), calls=%async_computation.3 | async-start | bytes 524288 | tf_op jit(solution)/shard_map/all_to_all | solution.py:118

commit v2 on v0

v2 whole, which is shorter than its diff:
```python
import jax
import jax.numpy as jnp
from jax import lax
from jax.experimental import pallas as pl
from jax.experimental.pallas import tpu as pltpu
from jax.sharding import PartitionSpec as P

BF16 = jnp.bfloat16
F32 = jnp.float32
UNROLL = 32
SMEM = pl.BlockSpec(memory_space=pltpu.SMEM)
VMEM = pl.BlockSpec(memory_space=pltpu.VMEM)
HBM = pl.BlockSpec(memory_space=pltpu.HBM)
PARAMS = pltpu.CompilerParams(vmem_limit_bytes=24 * 1024 * 1024)


def call(kernel, out, in_specs, name, scratch=()):
    return pl.pallas_call(
        kernel,
        out_shape=out,
        in_specs=in_specs,
        out_specs=jax.tree.map(lambda _: VMEM, out),
        scratch_shapes=list(scratch),
        compiler_params=PARAMS,
        name=name,
    )


def copies_kernel(x_ref, out_ref):
    for r in range(out_ref.shape[0]):
        out_ref[r] = x_ref[...]


def stage_kernel(vals_hbm, w_in, cot_in, vals_ref, wt_ref, parts_ref, sems):
    n = sems.shape[0]
    per = vals_ref.shape[0] // n
    copies = [
        pltpu.make_async_copy(
            vals_hbm.at[pl.ds(i * per, per)], vals_ref.at[pl.ds(i * per, per)], sems.at[i]
        )
        for i in range(n)
    ]
    for copy in copies:
        copy.start()
    wt_ref[...] = w_in[...].astype(F32).T.astype(wt_ref.dtype)
    tile = parts_ref.shape[2]
    for i in range(parts_ref.shape[0]):
        parts_ref[i] = cot_in[:, i * tile : (i + 1) * tile]
    for copy in copies:
        copy.wait()


def live_loop(count, products, add):
    def group(g, carry):
        first = g * UNROLL
        found = [products(first + u) for u in range(UNROLL)]
        for u in range(UNROLL):
            add(first + u, jnp.where(first + u < count, found[u], 0.0))
        return carry

    lax.fori_loop(0, (count + UNROLL - 1) // UNROLL, group, 0)


def aggregate_kernel(meta, x_ref, vals_ref, out_ref, acc):
    listed, tile = vals_ref.shape[:2]
    per = x_ref.shape[2] // tile
    acc[...] = jnp.zeros_like(acc)

    def product(t):
        at = meta[listed + t]
        start = pl.multiple_of((at % per) * tile, tile)
        return lax.dot_general(
            x_ref[at // per, :, pl.ds(start, tile)],
            vals_ref[t],
            (((1,), (1,)), ((), ())),
            preferred_element_type=F32,
        )

    def add(t, found):
        acc[meta[t]] = acc[meta[t]] + found

    live_loop(meta[2 * listed], product, add)
    out_ref[...] = acc[...].astype(out_ref.dtype)


def spread_kernel(part_ref, out_ref):
    total = jnp.sum(part_ref[...].astype(F32), axis=0).astype(out_ref.dtype)
    for i in range(out_ref.shape[0]):
        out_ref[i] = total


def middle_kernel(meta, h_ref, wt_ref, cot_ref, y_ref, terms_ref, grad_ref):
    groups, rows, tile = h_ref.shape
    tiles, outs = cot_ref.shape[:2]
    feat = rows // tiles
    wt = wt_ref[pl.ds(pl.multiple_of(meta[meta.shape[0] - 1] * outs, outs), outs), :]
    grad = jnp.zeros(grad_ref.shape, F32)
    for i in range(tiles):
        at = slice(i * tile, (i + 1) * tile)
        rows_at = slice(i * feat, (i + 1) * feat)
        h = h_ref[:, rows_at, :].reshape(groups * feat, tile)
        pre = jnp.dot(wt, h, preferred_element_type=F32)
        sig = jax.nn.sigmoid(pre)
        y_ref[:, at] = (pre * sig).astype(y_ref.dtype)
        dpre = (cot_ref[i].astype(F32) * sig * (1.0 + pre * (1.0 - sig))).astype(BF16)
        terms = lax.dot_general(
            wt, dpre, (((0,), (0,)), ((), ())), preferred_element_type=F32
        )
        terms_ref[:, rows_at, :] = terms.astype(terms_ref.dtype).reshape(groups, feat, tile)
        grad += lax.dot_general(
            dpre, h, (((1,), (1,)), ((), ())), preferred_element_type=F32
        )
    grad_ref[...] = grad.astype(grad_ref.dtype)


def pack_kernel(terms_ref, grad_ref, out_ref):
    total = jnp.sum(terms_ref[...].astype(F32), axis=0).astype(out_ref.dtype)
    rows = total.shape[0]
    for i in range(out_ref.shape[0]):
        out_ref[i, :rows] = total
        out_ref[i, rows:] = grad_ref[...]


def backward_kernel(meta, d_ref, vals_ref, out_ref, acc):
    listed = vals_ref.shape[0]
    parts, rows, tile = out_ref.shape
    per = acc.shape[0] // parts
    feat = acc.shape[1]
    slab_rows = per * feat
    acc[...] = jnp.zeros_like(acc)

    def product(t):
        at = meta[t]
        start = pl.multiple_of((at % per) * feat, feat)
        return jnp.dot(
            d_ref[at // per, pl.ds(start, feat), :], vals_ref[t], preferred_element_type=F32
        )

    def add(t, found):
        at = meta[listed + t]
        acc[at] = acc[at] + found

    live_loop(meta[2 * listed], product, add)
    grad = jnp.sum(d_ref[:, slab_rows:, :].astype(F32), axis=0).astype(out_ref.dtype)
    for r in range(parts):
        out_ref[r, :slab_rows] = (
            acc[r * per : (r + 1) * per].reshape(slab_rows, tile).astype(out_ref.dtype)
        )
        out_ref[r, slab_rows:] = grad


def final_kernel(in_ref, dx_ref, grad_ref):
    feat = dx_ref.shape[0]
    tile = in_ref.shape[2]
    slab_rows = in_ref.shape[1] - grad_ref.shape[0]
    for i in range(slab_rows // feat):
        dx_ref[:, i * tile : (i + 1) * tile] = jnp.sum(
            in_ref[:, i * feat : (i + 1) * feat, :].astype(F32), axis=0
        )
    grad_ref[...] = jnp.sum(in_ref[:, slab_rows:, :].astype(F32), axis=0)


def exchange(parts, axis):
    return lax.all_to_all(parts, axis, 0, 0, tiled=True)


def local(x_t, weight, cotangent_t, tile_vals, tile_rows, tile_cols, tile_count):
    feat, slab = x_t.shape
    tile = tile_vals.shape[-1]
    listed = tile_vals.shape[2]
    per = slab // tile
    n_row, n_col, n_rep = lax.axis_size("row"), lax.axis_size("col"), lax.axis_size("rep")
    rep_at = lax.axis_index("rep")
    out_loc = weight.shape[1] // n_rep
    grad_shape = (out_loc, n_rep * feat)
    shape = jax.ShapeDtypeStruct

    meta = jnp.concatenate(
        [tile_rows[0, 0], tile_cols[0, 0], tile_count[0], rep_at.reshape(1)]
    )

    x_parts = call(copies_kernel, shape((n_row, feat, slab), BF16), [VMEM], "copies")(x_t)
    x_all = exchange(x_parts, "row")
    vals, wt, cot = call(
        stage_kernel,
        (
            shape((listed, tile, tile), BF16),
            shape(weight.shape[::-1], BF16),
            shape((n_rep, out_loc, tile), BF16),
        ),
        [HBM, VMEM, VMEM],
        "stage",
        [pltpu.SemaphoreType.DMA((8,))],
    )(tile_vals[0, 0], weight, cotangent_t)

    part = call(
        aggregate_kernel,
        shape((n_col * per, feat, tile), BF16),
        [SMEM, VMEM, VMEM],
        "aggregate",
        [pltpu.VMEM((n_col * per, feat, tile), F32)],
    )(meta, x_all, vals)
    part = exchange(part.reshape(n_col, per * feat, tile), "col")

    mine = call(spread_kernel, shape((n_rep, per * feat, tile), BF16), [VMEM], "spread")(part)
    h_all = exchange(mine, "rep")

    y, terms, grad = call(
        middle_kernel,
        (
            shape((out_loc, slab), BF16),
            shape((n_rep, per * feat, tile), BF16),
            shape(grad_shape, BF16),
        ),
        [SMEM, VMEM, VMEM, VMEM],
        "middle",
    )(meta, h_all, wt, cot)
    terms = exchange(terms, "rep")
    send = call(
        pack_kernel, shape((n_col, per * feat + out_loc, tile), BF16), [VMEM, VMEM], "pack"
    )(terms, grad)
    d_all = exchange(send, "col")

    back = call(
        backward_kernel,
        shape((n_row, per * feat + out_loc, tile), BF16),
        [SMEM, VMEM, VMEM],
        "backward",
        [pltpu.VMEM((n_row * per, feat, tile), F32)],
    )(meta, d_all, vals)
    back = exchange(back, "row")

    dx, grad = call(
        final_kernel, (shape((feat, slab), F32), shape(grad_shape, F32)), [VMEM], "final"
    )(back)
    return y, dx, grad.T


def solution(mesh):
    return jax.shard_map(
        local,
        mesh=mesh,
        in_specs=(
            P("rep", ("row", "col")),
            P(),
            P("rep", ("row", "col")),
            P("row", "col", None, None, None),
            P("row", "col", None),
            P("row", "col", None),
            P("row", "col"),
        ),
        out_specs=(P("rep", ("row", "col")), P("rep", ("row", "col")), P(None, "rep")),
        check_vma=False,
    )
```

time: 579 us -> 121 us (0.21)
  the two profiles are of different devices: /device:TPU:32 before, /device:TPU:1 now
where the time goes in v2:
time: 121 us
  blocking collectives  89.9 us (74%)
  starting transfers between devices  9.24 us (8%)
  Pallas kernels  8.5 us (7%)
  waiting for transfers between devices  7.17 us (6%)
  local copies, waits for them, and re-layouts  4.32 us (4%)
  between operations  1.36 us (1%)
    all_to_all x5, blocking collectives, exchange(): return lax.all_to_all(parts, axis, 0, 0, tiled=True)  89.9 us
    all_to_all x1, starting transfers between devices, exchange(): return lax.all_to_all(parts, axis, 0, 0, tiled=True)  9.24 us
    all_to_all x1, waiting for transfers between devices, exchange(): return lax.all_to_all(parts, axis, 0, 0, tiled=True)  7.17 us
    unnamed x12, local copies, waits for them, and re-layouts  4.32 us
  transfers between devices with their start and end apart: 1, of which 1 were waited for; matrix products, arithmetic and copies ran while one was open for 0% of the time, Pallas kernels for 1%

profile of v2, /device:TPU:1, one launch (start us, length us, event | category | flops | bytes accessed | tf_op | source)
XLA Modules:
  0.0 120.6 jit_solution(5116767153701143239)
XLA Ops:
  0.6 0.0 copy-start.3
  0.6 0.7 copy-done.3
  1.4 0.0 copy-start.4
  1.4 0.0 copy-start.5
  1.4 0.8 copies.1
  2.2 9.2 %all-to-all-start = ((bf16[16,16,1024]{2,1,0:T(8,128)(2,1)}), bf16[16,16,1024]{2,1,0:T(8,128)(2,1)}, u32[]{:S(2)}, u32[]{:S(2)}) async-start(bf16[16,16,1024]{2,1,0:T(8,128)(2,1)} %copies.1), calls=%async_computation | async-start | bytes 1048576 | tf_op jit(solution)/shard_map/all_to_all | solution.py:164
  12.1 0.0 copy-start
  12.1 1.9 %copy-done = bf16[1,1,96,128,128]{4,3,2,1,0:T(8,128)(2,1)S(1)} copy-done((bf16[1,1,96,128,128]{4,3,2,1,0:T(8,128)(2,1)S(1)}, bf16[1,1,96,128,128]{4,3,2,1,0:T(8,128)(2,1)}, u32[]{:S(2)}) %copy-start) | copy-done | bytes 3145752
  14.0 0.8 copy-done.1
  14.8 0.8 copy-done.2
  15.7 1.7 %stage.1 = (bf16[96,128,128]{2,1,0:T(8,128)(2,1)S(1)}, bf16[256,128]{1,0:T(8,128)(2,1)S(1)}, bf16[8,32,128]{2,1,0:T(8,128)(2,1)S(1)}) custom-call(bf16[96,128,128]{2,1,0:T(8,128)(2,1)S(1)} %bitcast.8, bf16[128,256]{1,0:T(8,128)(2,1)S(1)} %copy-done.1, bf16[32,1024]{1,0:T(8,128)(2,1)S(1)} %copy-done.2), custom_call_target="tpu_custom_call" | custom-call | tf_op jit(solution)/shard_map/stage/pallas_call | solution.py:184
  17.4 0.0 copy-done.4
  17.4 0.0 copy-done.5
  17.4 0.1 pad_add_fusion.meta
  17.5 7.2 %all-to-all-done.x_ref = bf16[16,16,1024]{2,1,0:T(8,128)(2,1)} async-done(((bf16[16,16,1024]{2,1,0:T(8,128)(2,1)}), bf16[16,16,1024]{2,1,0:T(8,128)(2,1)}, u32[]{:S(2)}, u32[]{:S(2)}) %all-to-all-start) | async-done | bytes 524320 | tf_op jit(solution)/shard_map/all_to_all | solution.py:164
  24.6 1.7 %aggregate.1 = bf16[32,16,128]{2,1,0:T(8,128)(2,1)S(1)} custom-call(s32[194]{0:T(256)S(1)} %pad_add_fusion.meta, bf16[16,16,1024]{2,1,0:T(8,128)(2,1)} %all-to-all-done.x_ref, bf16[96,128,128]{2,1,0:T(8,128)(2,1)S(1)} %get-tuple-element.11.vals_ref), custom_call_target="tpu_custom_call" | custom-call | tf_op jit(solution)/shard_map/aggregate/pallas_call | solution.py:196
  26.4 24.7 %all_to_all.30.part_ref = bf16[4,128,128]{2,1,0:T(8,128)(2,1)S(1)} all-to-all(bf16[4,128,128]{2,1,0:T(8,128)(2,1)S(1)} %bitcast.9), channel_id=1, replica_groups=mesh['row'=16,'col'=4,'rep'=8] {'col'}, dimensions={0} | all-to-all | bytes 262144 | tf_op jit(solution)/shard_map/all_to_all | solution.py:164
  51.1 14.8 %all_to_all.31.h_ref = bf16[8,128,128]{2,1,0:T(8,128)(2,1)S(1)} all-to-all(bf16[8,128,128]{2,1,0:T(8,128)(2,1)S(1)} %spread.1), channel_id=1, replica_groups=mesh['row'=16,'col'=4,'rep'=8] {'rep'}, dimensions={0} | all-to-all | bytes 524288 | tf_op jit(solution)/shard_map/all_to_all | solution.py:164
  66.0 2.4 %middle.1 = (bf16[32,1024]{1,0:T(8,128)(2,1)}, bf16[8,128,128]{2,1,0:T(8,128)(2,1)S(1)}, bf16[32,128]{1,0:T(8,128)(2,1)S(1)}) custom-call(s32[194]{0:T(256)S(1)} %pad_add_fusion.meta, bf16[8,128,128]{2,1,0:T(8,128)(2,1)S(1)} %all_to_all.31.h_ref, bf16[256,128]{1,0:T(8,128)(2,1)S(1)} %get-tuple-element.12.wt_ref, ...), custom_call_target="tpu_custom_call" | custom-call | tf_op jit(solution)/shard_map/middle/pallas_call | solution.py:208
  68.4 9.9 %all_to_all.32.terms_ref = bf16[8,128,128]{2,1,0:T(8,128)(2,1)S(1)} all-to-all(bf16[8,128,128]{2,1,0:T(8,128)(2,1)S(1)} %get-tuple-element.15), channel_id=1, replica_groups=mesh['row'=16,'col'=4,'rep'=8] {'rep'}, dimensions={0} | all-to-all | bytes 524288 | tf_op jit(solution)/shard_map/all_to_all | solution.py:164
  78.3 15.6 %all_to_all.33.d_ref = bf16[4,160,128]{2,1,0:T(8,128)(2,1)S(1)} all-to-all(bf16[4,160,128]{2,1,0:T(8,128)(2,1)S(1)} %pack.1), channel_id=1, replica_groups=mesh['row'=16,'col'=4,'rep'=8] {'col'}, dimensions={0} | all-to-all | bytes 327680 | tf_op jit(solution)/shard_map/all_to_all | solution.py:164
  93.9 1.1 backward.1
  95.0 24.9 %all_to_all.34.in_ref = bf16[16,160,128]{2,1,0:T(8,128)(2,1)S(1)} all-to-all(bf16[16,160,128]{2,1,0:T(8,128)(2,1)S(1)} %backward.1), channel_id=1, replica_groups=mesh['row'=16,'col'=4,'rep'=8] {'row'}, dimensions={0} | all-to-all | bytes 1310720 | tf_op jit(solution)/shard_map/all_to_all | solution.py:164
  119.9 0.7 final.1
  (4 shorter events, 0.1 us)
Async XLA Ops:
  0.6 0.8 copy-start.3
  1.4 16.0 %copy-start.4 = (s32[1,1,96]{2,1,0:T(1,128)S(1)}, s32[1,1,96]{2,1,0:T(1,128)}, u32[]{:S(2)}) copy-start(s32[1,1,96]{2,1,0:T(1,128)} %param.12) | copy-start | bytes 1156
  1.4 16.0 %copy-start.5 = (s32[1,1,96]{2,1,0:T(1,128)S(1)}, s32[1,1,96]{2,1,0:T(1,128)}, u32[]{:S(2)}) copy-start(s32[1,1,96]{2,1,0:T(1,128)} %param.11) | copy-start | bytes 1156
  2.2 22.4 %all-to-all-start = ((bf16[16,16,1024]{2,1,0:T(8,128)(2,1)}), bf16[16,16,1024]{2,1,0:T(8,128)(2,1)}, u32[]{:S(2)}, u32[]{:S(2)}) async-start(bf16[16,16,1024]{2,1,0:T(8,128)(2,1)} %copies.1), calls=%async_computation | async-start | bytes 1048576 | tf_op jit(solution)/shard_map/all_to_all | solution.py:164
  12.1 1.9 %copy-start = (bf16[1,1,96,128,128]{4,3,2,1,0:T(8,128)(2,1)S(1)}, bf16[1,1,96,128,128]{4,3,2,1,0:T(8,128)(2,1)}, u32[]{:S(2)}) copy-start(bf16[1,1,96,128,128]{4,3,2,1,0:T(8,128)(2,1)} %param.10) | copy-start | bytes 9437188
  14.0 0.8 copy-start.1
  14.8 0.8 copy-start.2

commit v3 on v2

--- a/solution.py
+++ b/solution.py
@@ -31,7 +31,7 @@
         out_ref[r] = x_ref[...]
 
 
-def stage_kernel(vals_hbm, w_in, cot_in, vals_ref, wt_ref, parts_ref, sems):
+def stage_kernel(vals_hbm, vals_ref, sems):
     n = sems.shape[0]
     per = vals_ref.shape[0] // n
     copies = [
@@ -42,12 +42,17 @@
     ]
     for copy in copies:
         copy.start()
-    wt_ref[...] = w_in[...].astype(F32).T.astype(wt_ref.dtype)
-    tile = parts_ref.shape[2]
-    for i in range(parts_ref.shape[0]):
-        parts_ref[i] = cot_in[:, i * tile : (i + 1) * tile]
     for copy in copies:
         copy.wait()
+
+
+def cut_kernel(cot_ref, keep_ref, send_ref):
+    tile = keep_ref.shape[2]
+    me = lax.axis_index("rep")
+    for k in range(2 * keep_ref.shape[0]):
+        out_ref = send_ref if k % 2 else keep_ref
+        start = pl.multiple_of((me ^ k) * tile, tile)
+        out_ref[k // 2] = cot_ref[:, pl.ds(start, tile)]
 
 
 def live_loop(count, products, add):
@@ -83,42 +88,40 @@
     out_ref[...] = acc[...].astype(out_ref.dtype)
 
 
-def spread_kernel(part_ref, out_ref):
-    total = jnp.sum(part_ref[...].astype(F32), axis=0).astype(out_ref.dtype)
+def tile_kernel(part_ref, w_ref, low_ref, high_ref, out_ref, cot_all):
+    groups, _, tile = out_ref.shape
+    feat = part_ref.shape[1]
+    half, outs = low_ref.shape[:2]
+    me = lax.axis_index("rep")
+    for k in range(groups):
+        cot_all[me ^ k] = low_ref[k] if k < half else high_ref[k - half]
+    h = jnp.sum(
+        part_ref[...].reshape(-1, groups * feat, tile).astype(F32), axis=0
+    ).astype(BF16)
+    w = w_ref[...]
+    pre = lax.dot_general(w, h, (((0,), (0,)), ((), ())), preferred_element_type=F32)
+    sig = jax.nn.sigmoid(pre)
+    cot = cot_all[...].reshape(groups * outs, tile).astype(F32)
+    dpre = (cot * sig * (1.0 + pre * (1.0 - sig))).astype(BF16)
+    dagg = jnp.dot(w, dpre, preferred_element_type=F32)
+    grad = lax.dot_general(dpre, h, (((1,), (1,)), ((), ())), preferred_element_type=F32)
+    y = pre * sig
+    dtype = out_ref.dtype
+    out_ref[:, :feat] = dagg.astype(dtype).reshape(groups, feat, tile)
+    out_ref[:, feat : feat + outs] = y.astype(dtype).reshape(groups, outs, tile)
+    out_ref[:, feat + outs :] = grad.astype(dtype).reshape(groups, outs, tile)
+
+
+def pack_kernel(in_ref, out_ref):
+    tiles, in_rows, tile = in_ref.shape
+    outs = (in_rows * tiles - out_ref.shape[1]) // (2 * tiles - 1)
+    feat = in_rows - 2 * outs
+    rows = tiles * feat
+    dagg = in_ref[:, :feat].reshape(rows, tile)
+    grad = jnp.sum(in_ref[:, feat + outs :].astype(F32), axis=0).astype(out_ref.dtype)
     for i in range(out_ref.shape[0]):
-        out_ref[i] = total
-
-
-def middle_kernel(meta, h_ref, wt_ref, cot_ref, y_ref, terms_ref, grad_ref):
-    groups, rows, tile = h_ref.shape
-    tiles, outs = cot_ref.shape[:2]
-    feat = rows // tiles
-    wt = wt_ref[pl.ds(pl.multiple_of(meta[meta.shape[0] - 1] * outs, outs), outs), :]
-    grad = jnp.zeros(grad_ref.shape, F32)
-    for i in range(tiles):
-        at = slice(i * tile, (i + 1) * tile)
-        rows_at = slice(i * feat, (i + 1) * feat)
-        h = h_ref[:, rows_at, :].reshape(groups * feat, tile)
-        pre = jnp.dot(wt, h, preferred_element_type=F32)
-        sig = jax.nn.sigmoid(pre)
-        y_ref[:, at] = (pre * sig).astype(y_ref.dtype)
-        dpre = (cot_ref[i].astype(F32) * sig * (1.0 + pre * (1.0 - sig))).astype(BF16)
-        terms = lax.dot_general(
-            wt, dpre, (((0,), (0,)), ((), ())), preferred_element_type=F32
-        )
-        terms_ref[:, rows_at, :] = terms.astype(terms_ref.dtype).reshape(groups, feat, tile)
-        grad += lax.dot_general(
-            dpre, h, (((1,), (1,)), ((), ())), preferred_element_type=F32
-        )
-    grad_ref[...] = grad.astype(grad_ref.dtype)
-
-
-def pack_kernel(terms_ref, grad_ref, out_ref):
-    total = jnp.sum(terms_ref[...].astype(F32), axis=0).astype(out_ref.dtype)
-    rows = total.shape[0]
-    for i in range(out_ref.shape[0]):
-        out_ref[i, :rows] = total
-        out_ref[i, rows:] = grad_ref[...]
+        out_ref[i, :rows] = dagg
+        out_ref[i, rows:] = grad
 
 
 def backward_kernel(meta, d_ref, vals_ref, out_ref, acc):
@@ -149,7 +152,7 @@
         out_ref[r, slab_rows:] = grad
 
 
-def final_kernel(in_ref, dx_ref, grad_ref):
+def final_kernel(in_ref, mid_ref, dx_ref, y_ref, grad_ref):
     feat = dx_ref.shape[0]
     tile = in_ref.shape[2]
     slab_rows = in_ref.shape[1] - grad_ref.shape[0]
@@ -158,10 +161,18 @@
             in_ref[:, i * feat : (i + 1) * feat, :].astype(F32), axis=0
         )
     grad_ref[...] = jnp.sum(in_ref[:, slab_rows:, :].astype(F32), axis=0)
+    outs = y_ref.shape[0]
+    for i in range(mid_ref.shape[0]):
+        y_ref[:, i * tile : (i + 1) * tile] = mid_ref[i, feat : feat + outs]
 
 
 def exchange(parts, axis):
     return lax.all_to_all(parts, axis, 0, 0, tiled=True)
+
+
+def swap(parts, bit):
+    n = lax.axis_size("rep")
+    return lax.ppermute(parts, "rep", [(i, i ^ bit) for i in range(n)])
 
 
 def local(x_t, weight, cotangent_t, tile_vals, tile_rows, tile_cols, tile_count):
@@ -170,28 +181,33 @@
     listed = tile_vals.shape[2]
     per = slab // tile
     n_row, n_col, n_rep = lax.axis_size("row"), lax.axis_size("col"), lax.axis_size("rep")
-    rep_at = lax.axis_index("rep")
     out_loc = weight.shape[1] // n_rep
     grad_shape = (out_loc, n_rep * feat)
     shape = jax.ShapeDtypeStruct
 
-    meta = jnp.concatenate(
-        [tile_rows[0, 0], tile_cols[0, 0], tile_count[0], rep_at.reshape(1)]
-    )
+    meta = jnp.concatenate([tile_rows[0, 0], tile_cols[0, 0], tile_count[0]])
 
     x_parts = call(copies_kernel, shape((n_row, feat, slab), BF16), [VMEM], "copies")(x_t)
     x_all = exchange(x_parts, "row")
-    vals, wt, cot = call(
+    half = shape((n_rep // 2, out_loc, tile), BF16)
+    keep, send = call(cut_kernel, (half, half), [VMEM], "cut")(cotangent_t)
+    got = swap(send, 1)
+    keep, send = (
+        jnp.stack([keep[i], got[i], keep[i + 2], got[i + 2]]) for i in range(2)
+    )
+    got = swap(send, 2)
+    keep, send = (
+        jnp.stack([keep[i], keep[i + 1], got[i], got[i + 1]]) for i in (0, 2)
+    )
+    x_all, keep, send = lax.optimization_barrier((x_all, keep, send))
+    got = swap(send, 4)
+    vals = call(
         stage_kernel,
-        (
-            shape((listed, tile, tile), BF16),
-            shape(weight.shape[::-1], BF16),
-            shape((n_rep, out_loc, tile), BF16),
-        ),
-        [HBM, VMEM, VMEM],
+        shape((listed, tile, tile), BF16),
+        [HBM],
         "stage",
         [pltpu.SemaphoreType.DMA((8,))],
-    )(tile_vals[0, 0], weight, cotangent_t)
+    )(tile_vals[0, 0])
 
     part = call(
         aggregate_kernel,
@@ -200,25 +216,18 @@
         "aggregate",
         [pltpu.VMEM((n_col * per, feat, tile), F32)],
     )(meta, x_all, vals)
-    part = exchange(part.reshape(n_col, per * feat, tile), "col")
-
-    mine = call(spread_kernel, shape((n_rep, per * feat, tile), BF16), [VMEM], "spread")(part)
-    h_all = exchange(mine, "rep")
-
-    y, terms, grad = call(
-        middle_kernel,
-        (
-            shape((out_loc, slab), BF16),
-            shape((n_rep, per * feat, tile), BF16),
-            shape(grad_shape, BF16),
-        ),
-        [SMEM, VMEM, VMEM, VMEM],
-        "middle",
-    )(meta, h_all, wt, cot)
-    terms = exchange(terms, "rep")
-    send = call(
-        pack_kernel, shape((n_col, per * feat + out_loc, tile), BF16), [VMEM, VMEM], "pack"
-    )(terms, grad)
+    part = exchange(part, ("col", "rep"))
+
+    mid_rows = feat + 2 * out_loc
+    mid = call(
+        tile_kernel,
+        shape((n_rep, mid_rows, tile), BF16),
+        [VMEM] * 4,
+        "tile",
+        [pltpu.VMEM((n_rep, out_loc, tile), BF16)],
+    )(part, weight, keep, got)
+    mid = exchange(mid, "rep")
+    send = call(pack_kernel, shape((n_col, per * feat + out_loc, tile), BF16), [VMEM], "pack")(mid)
     d_all = exchange(send, "col")
 
     back = call(
@@ -230,9 +239,12 @@
     )(meta, d_all, vals)
     back = exchange(back, "row")
 
-    dx, grad = call(
-        final_kernel, (shape((feat, slab), F32), shape(grad_shape, F32)), [VMEM], "final"
-    )(back)
+    dx, y, grad = call(
+        final_kernel,
+        (shape((feat, slab), F32), shape((out_loc, slab), BF16), shape(grad_shape, F32)),
+        [VMEM, VMEM],
+        "final",
+    )(back, mid)
     return y, dx, grad.T
 
 

time: 121 us -> 115 us (0.950)
  blocking collectives: 89.9 us -> 49.9 us
  starting transfers between devices: 9.24 us -> 38.3 us
  waiting for transfers between devices: 7.17 us -> 13.6 us
  Pallas kernels: 8.5 us -> 7.05 us
    all_to_all x5 -> x3, blocking collectives: 89.9 us -> 49.9 us  [exchange(): return lax.all_to_all(parts, axis, 0, 0, tiled=True)]
    all_to_all x1 -> x2, starting transfers between devices: 9.24 us -> 27.5 us  [exchange(): return lax.all_to_all(parts, axis, 0, 0, tiled=True)]
    ppermute x0 -> x3, starting transfers between devices: none -> 10.8 us  [swap(): return lax.ppermute(parts, 'rep', [(i, i ^ bit) for i in range(n)])]
    all_to_all x1 -> x2, waiting for transfers between devices: 7.17 us -> 11.8 us  [exchange(): return lax.all_to_all(parts, axis, 0, 0, tiled=True)]
    pallas_call x4, Pallas kernels: 4.82 us -> 2.7 us  [the longest x1 1.57 us: local(): call(stage_kernel, shape((listed, tile, tile), BF16), [HBM], 'stage', [pl...]
    ppermute x0 -> x3, waiting for transfers between devices: none -> 1.83 us  [swap(): return lax.ppermute(parts, 'rep', [(i, i ^ bit) for i in range(n)])]
    unnamed x12 -> x8, local copies, waits for them, and re-layouts: 4.32 us -> 3.48 us
  transfers between devices with their start and end apart: 1 -> 5, of which waited for: 1 -> 4; matrix products, arithmetic and copies ran while one was open for 0% -> 1% of each run, Pallas kernels for 1% -> 1%
where the time goes in v3:
time: 115 us
  blocking collectives  49.9 us (43%)
  starting transfers between devices  38.3 us (33%)
  waiting for transfers between devices  13.6 us (12%)
  Pallas kernels  7.05 us (6%)
  local copies, waits for them, and re-layouts  3.5 us (3%)
  between operations  1.4 us (1%)
    all_to_all x3, blocking collectives, exchange(): return lax.all_to_all(parts, axis, 0, 0, tiled=True)  49.9 us
    all_to_all x2, starting transfers between devices, exchange(): return lax.all_to_all(parts, axis, 0, 0, tiled=True)  27.5 us
    all_to_all x2, waiting for transfers between devices, exchange(): return lax.all_to_all(parts, axis, 0, 0, tiled=True)  11.8 us
    ppermute x3, starting transfers between devices, swap(): return lax.ppermute(parts, 'rep', [(i, i ^ bit) for i in range(n)])  10.8 us
    unnamed x8, local copies, waits for them, and re-layouts  3.48 us
    pallas_call x1, Pallas kernels, local(): call(aggregate_kernel, shape((n_col * per, feat, tile), BF16), [SMEM, VME...  2.41 us
  transfers between devices with their start and end apart: 5, of which 4 were waited for; matrix products, arithmetic and copies ran while one was open for 1% of the time, Pallas kernels for 1%

profile of v3, /device:TPU:1, one launch (start us, length us, event | category | flops | bytes accessed | tf_op | source)
XLA Modules:
  0.0 114.5 jit_solution(15565840061572446544)
XLA Ops:
  0.6 0.7 copy-done.3
  1.4 0.8 copies.1
  2.2 9.2 %all-to-all-start = ((bf16[16,16,1024]{2,1,0:T(8,128)(2,1)}), bf16[16,16,1024]{2,1,0:T(8,128)(2,1)}, u32[]{:S(2)}, u32[]{:S(2)}) async-start(bf16[16,16,1024]{2,1,0:T(8,128)(2,1)} %copies.1), calls=%async_computation | async-start | bytes 1048576 | tf_op jit(solution)/shard_map/all_to_all | solution.py:170
  11.5 0.0 copy-start.1
  11.5 0.8 copy-done.1
  12.3 3.8 %collective-permute-start = (bf16[4,32,128]{2,1,0:T(8,128)(2,1)S(1)}, bf16[4,32,128]{2,1,0:T(8,128)(2,1)S(1)}, u32[]{:S(2)}, u32[]{:S(2)}) collective-permute-start(bf16[4,32,128]{2,1,0:T(8,128)(2,1)S(1)} %get-tuple-element.12), channel_id=1, source_target_pairs={{0,1},{1,0},{2,3},{3,2},{4,5},{5,4},{6,7},{7,6},{8,9},{9,8},{10,11... | collective-permute-start | bytes 98312 | tf_op jit(solution)/shard_map/ppermute | solution.py:175
  16.8 0.2 collective-permute-done
  17.0 2.2 %collective-permute-start.1 = (bf16[4,32,128]{2,1,0:T(8,128)(2,1)S(1)}, bf16[4,32,128]{2,1,0:T(8,128)(2,1)S(1)}, u32[]{:S(2)}, u32[]{:S(2)}) collective-permute-start(bf16[4,32,128]{2,1,0:T(8,128)(2,1)S(1)} %pad_maximum_fusion), channel_id=1, source_target_pairs={{0,2},{1,3},{2,0},{3,1},{4,6},{5,7},{6,4},{7,5},{8,10},{9,11},{10,... | collective-permute-start | bytes 98312 | tf_op jit(solution)/shard_map/ppermute | solution.py:175
  19.2 0.8 pad_add_fusion.meta
  19.9 1.9 %copy-done = bf16[1,1,96,128,128]{4,3,2,1,0:T(8,128)(2,1)S(1)} copy-done((bf16[1,1,96,128,128]{4,3,2,1,0:T(8,128)(2,1)S(1)}, bf16[1,1,96,128,128]{4,3,2,1,0:T(8,128)(2,1)}, u32[]{:S(2)}) %copy-start) | copy-done | bytes 3145752
  21.8 1.6 %stage.1.vals_ref = bf16[96,128,128]{2,1,0:T(8,128)(2,1)S(1)} custom-call(bf16[96,128,128]{2,1,0:T(8,128)(2,1)S(1)} %bitcast.6), custom_call_target="tpu_custom_call" | custom-call | tf_op jit(solution)/shard_map/stage/pallas_call | solution.py:204
  23.4 0.0 copy-start.2
  23.5 1.2 %all-to-all-done.x_ref = bf16[16,16,1024]{2,1,0:T(8,128)(2,1)} async-done(((bf16[16,16,1024]{2,1,0:T(8,128)(2,1)}), bf16[16,16,1024]{2,1,0:T(8,128)(2,1)}, u32[]{:S(2)}, u32[]{:S(2)}) %all-to-all-start) | async-done | bytes 524320 | tf_op jit(solution)/shard_map/all_to_all | solution.py:170
  24.7 2.4 %aggregate.1 = bf16[32,16,128]{2,1,0:T(8,128)(2,1)} custom-call(s32[193]{0:T(256)S(1)} %pad_add_fusion.meta, bf16[16,16,1024]{2,1,0:T(8,128)(2,1)} %all-to-all-done.x_ref, bf16[96,128,128]{2,1,0:T(8,128)(2,1)S(1)} %stage.1.vals_ref), custom_call_target="tpu_custom_call" | custom-call | tf_op jit(solution)/shard_map/aggregate/pallas_call | solution.py:212
  27.1 18.3 %all-to-all-start.1 = ((bf16[32,16,128]{2,1,0:T(8,128)(2,1)}), bf16[32,16,128]{2,1,0:T(8,128)(2,1)S(1)}, u32[]{:S(2)}, u32[]{:S(2)}) async-start(bf16[32,16,128]{2,1,0:T(8,128)(2,1)} %aggregate.1), calls=%async_computation.1 | async-start | bytes 262144 | tf_op jit(solution)/shard_map/all_to_all | solution.py:170
  45.4 4.8 %collective-permute-start.2 = (bf16[4,32,128]{2,1,0:T(8,128)(2,1)S(1)}, bf16[4,32,128]{2,1,0:T(8,128)(2,1)S(1)}, u32[]{:S(2)}, u32[]{:S(2)}) collective-permute-start(bf16[4,32,128]{2,1,0:T(8,128)(2,1)S(1)} %get-tuple-element.15), channel_id=1, source_target_pairs={{0,4},{1,5},{2,6},{3,7},{4,0},{5,1},{6,2},{7,3},{8,12},{9,13},{10,... | collective-permute-start | bytes 98312 | tf_op jit(solution)/shard_map/ppermute | solution.py:175
  50.2 1.7 %collective-permute-done.2.high_ref = bf16[4,32,128]{2,1,0:T(8,128)(2,1)S(1)} collective-permute-done((bf16[4,32,128]{2,1,0:T(8,128)(2,1)S(1)}, bf16[4,32,128]{2,1,0:T(8,128)(2,1)S(1)}, u32[]{:S(2)}, u32[]{:S(2)}) %collective-permute-start.2) | collective-permute-done | bytes 32800 | tf_op jit(solution)/shard_map/ppermute | solution.py:175
  51.8 10.6 %all-to-all-done.1.part_ref = bf16[32,16,128]{2,1,0:T(8,128)(2,1)S(1)} async-done(((bf16[32,16,128]{2,1,0:T(8,128)(2,1)}), bf16[32,16,128]{2,1,0:T(8,128)(2,1)S(1)}, u32[]{:S(2)}, u32[]{:S(2)}) %all-to-all-start.1) | async-done | bytes 131104 | tf_op jit(solution)/shard_map/all_to_all | solution.py:170
  62.4 0.4 tile.1
  62.8 8.2 %all_to_all.25.in_ref.mid_ref = bf16[8,80,128]{2,1,0:T(8,128)(2,1)S(1)} all-to-all(bf16[8,80,128]{2,1,0:T(8,128)(2,1)S(1)} %tile.1), channel_id=1, replica_groups=mesh['row'=16,'col'=4,'rep'=8] {'rep'}, dimensions={0} | all-to-all | bytes 327680 | tf_op jit(solution)/shard_map/all_to_all | solution.py:170
  71.0 17.0 %all_to_all.26.d_ref = bf16[4,160,128]{2,1,0:T(8,128)(2,1)S(1)} all-to-all(bf16[4,160,128]{2,1,0:T(8,128)(2,1)S(1)} %pack.1), channel_id=1, replica_groups=mesh['row'=16,'col'=4,'rep'=8] {'col'}, dimensions={0} | all-to-all | bytes 327680 | tf_op jit(solution)/shard_map/all_to_all | solution.py:170
  88.0 1.1 backward.1
  89.1 24.7 %all_to_all.27.in_ref = bf16[16,160,128]{2,1,0:T(8,128)(2,1)S(1)} all-to-all(bf16[16,160,128]{2,1,0:T(8,128)(2,1)S(1)} %backward.1), channel_id=1, replica_groups=mesh['row'=16,'col'=4,'rep'=8] {'row'}, dimensions={0} | all-to-all | bytes 1310720 | tf_op jit(solution)/shard_map/all_to_all | solution.py:170
  113.8 0.7 final.1
  (11 shorter events, 0.1 us)
Async XLA Ops:
  0.6 0.8 copy-start.3
  2.2 22.4 %all-to-all-start = ((bf16[16,16,1024]{2,1,0:T(8,128)(2,1)}), bf16[16,16,1024]{2,1,0:T(8,128)(2,1)}, u32[]{:S(2)}, u32[]{:S(2)}) async-start(bf16[16,16,1024]{2,1,0:T(8,128)(2,1)} %copies.1), calls=%async_computation | async-start | bytes 1048576 | tf_op jit(solution)/shard_map/all_to_all | solution.py:170
  11.5 0.8 copy-start.1
  12.3 4.6 %collective-permute-start = (bf16[4,32,128]{2,1,0:T(8,128)(2,1)S(1)}, bf16[4,32,128]{2,1,0:T(8,128)(2,1)S(1)}, u32[]{:S(2)}, u32[]{:S(2)}) collective-permute-start(bf16[4,32,128]{2,1,0:T(8,128)(2,1)S(1)} %get-tuple-element.12), channel_id=1, source_target_pairs={{0,1},{1,0},{2,3},{3,2},{4,5},{5,4},{6,7},{7,6},{8,9},{9,8},{10,11... | collective-permute-start | bytes 98312 | tf_op jit(solution)/shard_map/ppermute | solution.py:175
  17.0 6.4 %collective-permute-start.1 = (bf16[4,32,128]{2,1,0:T(8,128)(2,1)S(1)}, bf16[4,32,128]{2,1,0:T(8,128)(2,1)S(1)}, u32[]{:S(2)}, u32[]{:S(2)}) collective-permute-start(bf16[4,32,128]{2,1,0:T(8,128)(2,1)S(1)} %pad_maximum_fusion), channel_id=1, source_target_pairs={{0,2},{1,3},{2,0},{3,1},{4,6},{5,7},{6,4},{7,5},{8,10},{9,11},{10,... | collective-permute-start | bytes 98312 | tf_op jit(solution)/shard_map/ppermute | solution.py:175
  19.9 1.9 %copy-start = (bf16[1,1,96,128,128]{4,3,2,1,0:T(8,128)(2,1)S(1)}, bf16[1,1,96,128,128]{4,3,2,1,0:T(8,128)(2,1)}, u32[]{:S(2)}) copy-start(bf16[1,1,96,128,128]{4,3,2,1,0:T(8,128)(2,1)} %param.10) | copy-start | bytes 9437188
  23.4 39.0 %copy-start.2 = (bf16[128,256]{1,0:T(8,128)(2,1)S(1)}, bf16[128,256]{1,0:T(8,128)(2,1)}, u32[]{:S(2)}) copy-start(bf16[128,256]{1,0:T(8,128)(2,1)} %w_ref.1) | copy-start | bytes 196612
  27.1 35.3 %all-to-all-start.1 = ((bf16[32,16,128]{2,1,0:T(8,128)(2,1)}), bf16[32,16,128]{2,1,0:T(8,128)(2,1)S(1)}, u32[]{:S(2)}, u32[]{:S(2)}) async-start(bf16[32,16,128]{2,1,0:T(8,128)(2,1)} %aggregate.1), calls=%async_computation.1 | async-start | bytes 262144 | tf_op jit(solution)/shard_map/all_to_all | solution.py:170
  45.4 6.5 %collective-permute-start.2 = (bf16[4,32,128]{2,1,0:T(8,128)(2,1)S(1)}, bf16[4,32,128]{2,1,0:T(8,128)(2,1)S(1)}, u32[]{:S(2)}, u32[]{:S(2)}) collective-permute-start(bf16[4,32,128]{2,1,0:T(8,128)(2,1)S(1)} %get-tuple-element.15), channel_id=1, source_target_pairs={{0,4},{1,5},{2,6},{3,7},{4,0},{5,1},{6,2},{7,3},{8,12},{9,13},{10,... | collective-permute-start | bytes 98312 | tf_op jit(solution)/shard_map/ppermute | solution.py:175

commit v4 on v3

--- a/solution.py
+++ b/solution.py
@@ -1,3 +1,5 @@
+import functools
+
 import jax
 import jax.numpy as jnp
 from jax import lax
@@ -66,7 +68,7 @@
     lax.fori_loop(0, (count + UNROLL - 1) // UNROLL, group, 0)
 
 
-def aggregate_kernel(meta, x_ref, vals_ref, out_ref, acc):
+def aggregate_kernel(row_turn, turn, meta, x_ref, vals_ref, out_ref, acc):
     listed, tile = vals_ref.shape[:2]
     per = x_ref.shape[2] // tile
     acc[...] = jnp.zeros_like(acc)
@@ -75,7 +77,7 @@
         at = meta[listed + t]
         start = pl.multiple_of((at % per) * tile, tile)
         return lax.dot_general(
-            x_ref[at // per, :, pl.ds(start, tile)],
+            x_ref[turned_at(at // per, row_turn, x_ref.shape[0]), :, pl.ds(start, tile)],
             vals_ref[t],
             (((1,), (1,)), ((), ())),
             preferred_element_type=F32,
@@ -85,7 +87,9 @@
         acc[meta[t]] = acc[meta[t]] + found
 
     live_loop(meta[2 * listed], product, add)
-    out_ref[...] = acc[...].astype(out_ref.dtype)
+    cut = turn * per
+    out_ref[: acc.shape[0] - cut] = acc[cut:].astype(out_ref.dtype)
+    out_ref[acc.shape[0] - cut :] = acc[:cut].astype(out_ref.dtype)
 
 
 def tile_kernel(part_ref, w_ref, low_ref, high_ref, out_ref, cot_all):
@@ -124,7 +128,7 @@
         out_ref[i, rows:] = grad
 
 
-def backward_kernel(meta, d_ref, vals_ref, out_ref, acc):
+def backward_kernel(row_turn, turn, meta, d_ref, vals_ref, out_ref, acc):
     listed = vals_ref.shape[0]
     parts, rows, tile = out_ref.shape
     per = acc.shape[0] // parts
@@ -136,7 +140,9 @@
         at = meta[t]
         start = pl.multiple_of((at % per) * feat, feat)
         return jnp.dot(
-            d_ref[at // per, pl.ds(start, feat), :], vals_ref[t], preferred_element_type=F32
+            d_ref[turned_at(at // per, turn, d_ref.shape[0]), pl.ds(start, feat), :],
+            vals_ref[t],
+            preferred_element_type=F32,
         )
 
     def add(t, found):
@@ -145,11 +151,12 @@
 
     live_loop(meta[2 * listed], product, add)
     grad = jnp.sum(d_ref[:, slab_rows:, :].astype(F32), axis=0).astype(out_ref.dtype)
-    for r in range(parts):
-        out_ref[r, :slab_rows] = (
+    for i in range(parts):
+        r = (i + row_turn) % parts
+        out_ref[i, :slab_rows] = (
             acc[r * per : (r + 1) * per].reshape(slab_rows, tile).astype(out_ref.dtype)
         )
-        out_ref[r, slab_rows:] = grad
+        out_ref[i, slab_rows:] = grad
 
 
 def final_kernel(in_ref, mid_ref, dx_ref, y_ref, grad_ref):
@@ -166,8 +173,14 @@
         y_ref[:, i * tile : (i + 1) * tile] = mid_ref[i, feat : feat + outs]
 
 
-def exchange(parts, axis):
-    return lax.all_to_all(parts, axis, 0, 0, tiled=True)
+def turned_at(member, turn, n):
+    return (member + n - turn) % n
+
+
+def exchange(parts, axis, turn=0):
+    n = lax.axis_size(axis)
+    groups = [[(i + turn) % n for i in range(n)]] if turn else None
+    return lax.all_to_all(parts, axis, 0, 0, axis_index_groups=groups, tiled=True)
 
 
 def swap(parts, bit):
@@ -182,13 +195,14 @@
     per = slab // tile
     n_row, n_col, n_rep = lax.axis_size("row"), lax.axis_size("col"), lax.axis_size("rep")
     out_loc = weight.shape[1] // n_rep
+    row_turn, col_turn = n_row // 4, n_col // 2
     grad_shape = (out_loc, n_rep * feat)
     shape = jax.ShapeDtypeStruct
 
     meta = jnp.concatenate([tile_rows[0, 0], tile_cols[0, 0], tile_count[0]])
 
     x_parts = call(copies_kernel, shape((n_row, feat, slab), BF16), [VMEM], "copies")(x_t)
-    x_all = exchange(x_parts, "row")
+    x_all = exchange(x_parts, "row", row_turn)
     half = shape((n_rep // 2, out_loc, tile), BF16)
     keep, send = call(cut_kernel, (half, half), [VMEM], "cut")(cotangent_t)
     got = swap(send, 1)
@@ -210,13 +224,13 @@
     )(tile_vals[0, 0])
 
     part = call(
-        aggregate_kernel,
+        functools.partial(aggregate_kernel, row_turn, col_turn),
         shape((n_col * per, feat, tile), BF16),
         [SMEM, VMEM, VMEM],
         "aggregate",
         [pltpu.VMEM((n_col * per, feat, tile), F32)],
     )(meta, x_all, vals)
-    part = exchange(part, ("col", "rep"))
+    part = exchange(part, ("col", "rep"), col_turn * n_rep)
 
     mid_rows = feat + 2 * out_loc
     mid = call(
@@ -228,16 +242,16 @@
     )(part, weight, keep, got)
     mid = exchange(mid, "rep")
     send = call(pack_kernel, shape((n_col, per * feat + out_loc, tile), BF16), [VMEM], "pack")(mid)
-    d_all = exchange(send, "col")
+    d_all = exchange(send, "col", col_turn)
 
     back = call(
-        backward_kernel,
+        functools.partial(backward_kernel, row_turn, col_turn),
         shape((n_row, per * feat + out_loc, tile), BF16),
         [SMEM, VMEM, VMEM],
         "backward",
         [pltpu.VMEM((n_row * per, feat, tile), F32)],
     )(meta, d_all, vals)
-    back = exchange(back, "row")
+    back = exchange(back, "row", row_turn)
 
     dx, y, grad = call(
         final_kernel,

time: 115 us -> 107 us (0.930)
  waiting for transfers between devices: 13.6 us -> 5.39 us
  blocking collectives: 49.9 us -> 46.6 us
  starting transfers between devices: 38.3 us -> 41.2 us
    all_to_all x2, waiting for transfers between devices: 11.8 us -> 3.27 us  [exchange(): lax.all_to_all(parts, axis, 0, 0, axis_index_groups=groups, tiled=True)]
    all_to_all x3, blocking collectives: 49.9 us -> 46.6 us  [exchange(): lax.all_to_all(parts, axis, 0, 0, axis_index_groups=groups, tiled=True)]
    all_to_all x2, starting transfers between devices: 27.5 us -> 30.4 us  [exchange(): lax.all_to_all(parts, axis, 0, 0, axis_index_groups=groups, tiled=True)]
where the time goes in v4:
time: 107 us; the launch traced here: 106 us
  blocking collectives  46.6 us (44%)
  starting transfers between devices  41.2 us (39%)
  Pallas kernels  7.11 us (7%)
  waiting for transfers between devices  5.39 us (5%)
  local copies, waits for them, and re-layouts  3.49 us (3%)
  between operations  1.4 us (1%)
    all_to_all x3, blocking collectives, exchange(): lax.all_to_all(parts, axis, 0, 0, axis_index_groups=groups, tiled=True)  46.6 us
    all_to_all x2, starting transfers between devices, exchange(): lax.all_to_all(parts, axis, 0, 0, axis_index_groups=groups, tiled=True)  30.4 us
    ppermute x3, starting transfers between devices, swap(): return lax.ppermute(parts, 'rep', [(i, i ^ bit) for i in range(n)])  10.9 us
    unnamed x8, local copies, waits for them, and re-layouts  3.48 us
    all_to_all x2, waiting for transfers between devices, exchange(): lax.all_to_all(parts, axis, 0, 0, axis_index_groups=groups, tiled=True)  3.27 us
    pallas_call x1, Pallas kernels, local(): call(functools.partial(aggregate_kernel, row_turn, col_turn), shape((n_co...  2.41 us
  transfers between devices with their start and end apart: 5, of which 4 were waited for; matrix products, arithmetic and copies ran while one was open for 1% of the time, Pallas kernels for 1%

profile of v4, /device:TPU:1, one launch (start us, length us, event | category | flops | bytes accessed | tf_op | source)
XLA Modules:
  0.0 106.0 jit_solution(8720653380889538515)
XLA Ops:
  0.6 0.7 copy-done.3
  1.4 0.8 copies.1
  2.2 9.4 %all-to-all-start = ((bf16[16,16,1024]{2,1,0:T(8,128)(2,1)}), bf16[16,16,1024]{2,1,0:T(8,128)(2,1)}, u32[]{:S(2)}, u32[]{:S(2)}) async-start(bf16[16,16,1024]{2,1,0:T(8,128)(2,1)} %copies.1), calls=%async_computation | async-start | bytes 1048576 | tf_op jit(solution)/shard_map/all_to_all | solution.py:183
  11.6 0.8 copy-done.1
  12.5 3.6 %collective-permute-start = (bf16[4,32,128]{2,1,0:T(8,128)(2,1)S(1)}, bf16[4,32,128]{2,1,0:T(8,128)(2,1)S(1)}, u32[]{:S(2)}, u32[]{:S(2)}) collective-permute-start(bf16[4,32,128]{2,1,0:T(8,128)(2,1)S(1)} %get-tuple-element.12), channel_id=1, source_target_pairs={{0,1},{1,0},{2,3},{3,2},{4,5},{5,4},{6,7},{7,6},{8,9},{9,8},{10,11... | collective-permute-start | bytes 98312 | tf_op jit(solution)/shard_map/ppermute | solution.py:188
  16.7 0.2 collective-permute-done
  16.9 2.7 %collective-permute-start.1 = (bf16[4,32,128]{2,1,0:T(8,128)(2,1)S(1)}, bf16[4,32,128]{2,1,0:T(8,128)(2,1)S(1)}, u32[]{:S(2)}, u32[]{:S(2)}) collective-permute-start(bf16[4,32,128]{2,1,0:T(8,128)(2,1)S(1)} %pad_maximum_fusion), channel_id=1, source_target_pairs={{0,2},{1,3},{2,0},{3,1},{4,6},{5,7},{6,4},{7,5},{8,10},{9,11},{10,... | collective-permute-start | bytes 98312 | tf_op jit(solution)/shard_map/ppermute | solution.py:188
  19.6 0.8 pad_add_fusion.meta
  20.4 1.9 %copy-done = bf16[1,1,96,128,128]{4,3,2,1,0:T(8,128)(2,1)S(1)} copy-done((bf16[1,1,96,128,128]{4,3,2,1,0:T(8,128)(2,1)S(1)}, bf16[1,1,96,128,128]{4,3,2,1,0:T(8,128)(2,1)}, u32[]{:S(2)}) %copy-start) | copy-done | bytes 3145752
  22.2 1.6 %stage.1.vals_ref = bf16[96,128,128]{2,1,0:T(8,128)(2,1)S(1)} custom-call(bf16[96,128,128]{2,1,0:T(8,128)(2,1)S(1)} %bitcast.6), custom_call_target="tpu_custom_call" | custom-call | tf_op jit(solution)/shard_map/stage/pallas_call | solution.py:218
  23.8 0.0 copy-start.2
  23.8 0.0 collective-permute-done.1
  23.9 0.5 all-to-all-done.x_ref
  24.4 2.4 %aggregate.1 = bf16[32,16,128]{2,1,0:T(8,128)(2,1)} custom-call(s32[193]{0:T(256)S(1)} %pad_add_fusion.meta, bf16[16,16,1024]{2,1,0:T(8,128)(2,1)} %all-to-all-done.x_ref, bf16[96,128,128]{2,1,0:T(8,128)(2,1)S(1)} %stage.1.vals_ref), custom_call_target="tpu_custom_call" | custom-call | tf_op jit(solution)/shard_map/aggregate/pallas_call | solution.py:226
  26.8 21.0 %all-to-all-start.1 = ((bf16[32,16,128]{2,1,0:T(8,128)(2,1)}), bf16[32,16,128]{2,1,0:T(8,128)(2,1)S(1)}, u32[]{:S(2)}, u32[]{:S(2)}) async-start(bf16[32,16,128]{2,1,0:T(8,128)(2,1)} %aggregate.1), calls=%async_computation.1 | async-start | bytes 262144 | tf_op jit(solution)/shard_map/all_to_all | solution.py:183
  47.8 4.6 %collective-permute-start.2 = (bf16[4,32,128]{2,1,0:T(8,128)(2,1)S(1)}, bf16[4,32,128]{2,1,0:T(8,128)(2,1)S(1)}, u32[]{:S(2)}, u32[]{:S(2)}) collective-permute-start(bf16[4,32,128]{2,1,0:T(8,128)(2,1)S(1)} %get-tuple-element.15), channel_id=1, source_target_pairs={{0,4},{1,5},{2,6},{3,7},{4,0},{5,1},{6,2},{7,3},{8,12},{9,13},{10,... | collective-permute-start | bytes 98312 | tf_op jit(solution)/shard_map/ppermute | solution.py:188
  52.4 1.9 %collective-permute-done.2.high_ref = bf16[4,32,128]{2,1,0:T(8,128)(2,1)S(1)} collective-permute-done((bf16[4,32,128]{2,1,0:T(8,128)(2,1)S(1)}, bf16[4,32,128]{2,1,0:T(8,128)(2,1)S(1)}, u32[]{:S(2)}, u32[]{:S(2)}) %collective-permute-start.2) | collective-permute-done | bytes 32800 | tf_op jit(solution)/shard_map/ppermute | solution.py:188
  54.4 2.8 %all-to-all-done.1.part_ref = bf16[32,16,128]{2,1,0:T(8,128)(2,1)S(1)} async-done(((bf16[32,16,128]{2,1,0:T(8,128)(2,1)}), bf16[32,16,128]{2,1,0:T(8,128)(2,1)S(1)}, u32[]{:S(2)}, u32[]{:S(2)}) %all-to-all-start.1) | async-done | bytes 131104 | tf_op jit(solution)/shard_map/all_to_all | solution.py:183
  57.1 0.4 tile.1
  57.5 8.0 %all_to_all.25.in_ref.mid_ref = bf16[8,80,128]{2,1,0:T(8,128)(2,1)S(1)} all-to-all(bf16[8,80,128]{2,1,0:T(8,128)(2,1)S(1)} %tile.1), channel_id=1, replica_groups=mesh['row'=16,'col'=4,'rep'=8] {'rep'}, dimensions={0} | all-to-all | bytes 327680 | tf_op jit(solution)/shard_map/all_to_all | solution.py:183
  65.5 17.8 %all_to_all.26.d_ref = bf16[4,160,128]{2,1,0:T(8,128)(2,1)S(1)} all-to-all(bf16[4,160,128]{2,1,0:T(8,128)(2,1)S(1)} %pack.1), channel_id=1, replica_groups={{16,24,0,8},{17,25,1,9},{18,26,2,10},{19,27,3,11},{20,28,4,12},{21,29,5..., dimensions={0} | all-to-all | bytes 327680 | tf_op jit(solution)/shard_map/all_to_all | solution.py:183
  83.3 1.2 %backward.1 = bf16[16,160,128]{2,1,0:T(8,128)(2,1)S(1)} custom-call(s32[193]{0:T(256)S(1)} %pad_add_fusion.meta, bf16[4,160,128]{2,1,0:T(8,128)(2,1)S(1)} %all_to_all.26.d_ref, bf16[96,128,128]{2,1,0:T(8,128)(2,1)S(1)} %stage.1.vals_ref), custom_call_target="tpu_custom_call" | custom-call | tf_op jit(solution)/shard_map/backward/pallas_call | solution.py:247
  84.5 20.8 %all_to_all.27.in_ref = bf16[16,160,128]{2,1,0:T(8,128)(2,1)S(1)} all-to-all(bf16[16,160,128]{2,1,0:T(8,128)(2,1)S(1)} %backward.1), channel_id=1, replica_groups={{128,160,192,224,256,288,320,352,384,416,448,480,0,32,64,96},{129,161,1..., dimensions={0} | all-to-all | bytes 1310720 | tf_op jit(solution)/shard_map/all_to_all | solution.py:183
  105.3 0.7 final.1
  (11 shorter events, 0.1 us)
Async XLA Ops:
  0.6 0.8 copy-start.3
  2.2 22.2 %all-to-all-start = ((bf16[16,16,1024]{2,1,0:T(8,128)(2,1)}), bf16[16,16,1024]{2,1,0:T(8,128)(2,1)}, u32[]{:S(2)}, u32[]{:S(2)}) async-start(bf16[16,16,1024]{2,1,0:T(8,128)(2,1)} %copies.1), calls=%async_computation | async-start | bytes 1048576 | tf_op jit(solution)/shard_map/all_to_all | solution.py:183
  11.6 0.8 copy-start.1
  12.5 4.4 %collective-permute-start = (bf16[4,32,128]{2,1,0:T(8,128)(2,1)S(1)}, bf16[4,32,128]{2,1,0:T(8,128)(2,1)S(1)}, u32[]{:S(2)}, u32[]{:S(2)}) collective-permute-start(bf16[4,32,128]{2,1,0:T(8,128)(2,1)S(1)} %get-tuple-element.12), channel_id=1, source_target_pairs={{0,1},{1,0},{2,3},{3,2},{4,5},{5,4},{6,7},{7,6},{8,9},{9,8},{10,11... | collective-permute-start | bytes 98312 | tf_op jit(solution)/shard_map/ppermute | solution.py:188
  16.9 7.0 %collective-permute-start.1 = (bf16[4,32,128]{2,1,0:T(8,128)(2,1)S(1)}, bf16[4,32,128]{2,1,0:T(8,128)(2,1)S(1)}, u32[]{:S(2)}, u32[]{:S(2)}) collective-permute-start(bf16[4,32,128]{2,1,0:T(8,128)(2,1)S(1)} %pad_maximum_fusion), channel_id=1, source_target_pairs={{0,2},{1,3},{2,0},{3,1},{4,6},{5,7},{6,4},{7,5},{8,10},{9,11},{10,... | collective-permute-start | bytes 98312 | tf_op jit(solution)/shard_map/ppermute | solution.py:188
  20.3 1.9 %copy-start = (bf16[1,1,96,128,128]{4,3,2,1,0:T(8,128)(2,1)S(1)}, bf16[1,1,96,128,128]{4,3,2,1,0:T(8,128)(2,1)}, u32[]{:S(2)}) copy-start(bf16[1,1,96,128,128]{4,3,2,1,0:T(8,128)(2,1)} %param.10) | copy-start | bytes 9437188
  23.8 33.3 %copy-start.2 = (bf16[128,256]{1,0:T(8,128)(2,1)S(1)}, bf16[128,256]{1,0:T(8,128)(2,1)}, u32[]{:S(2)}) copy-start(bf16[128,256]{1,0:T(8,128)(2,1)} %w_ref.1) | copy-start | bytes 196612
  26.8 30.3 %all-to-all-start.1 = ((bf16[32,16,128]{2,1,0:T(8,128)(2,1)}), bf16[32,16,128]{2,1,0:T(8,128)(2,1)S(1)}, u32[]{:S(2)}, u32[]{:S(2)}) async-start(bf16[32,16,128]{2,1,0:T(8,128)(2,1)} %aggregate.1), calls=%async_computation.1 | async-start | bytes 262144 | tf_op jit(solution)/shard_map/all_to_all | solution.py:183
  47.8 6.5 %collective-permute-start.2 = (bf16[4,32,128]{2,1,0:T(8,128)(2,1)S(1)}, bf16[4,32,128]{2,1,0:T(8,128)(2,1)S(1)}, u32[]{:S(2)}, u32[]{:S(2)}) collective-permute-start(bf16[4,32,128]{2,1,0:T(8,128)(2,1)S(1)} %get-tuple-element.15), channel_id=1, source_target_pairs={{0,4},{1,5},{2,6},{3,7},{4,0},{5,1},{6,2},{7,3},{8,12},{9,13},{10,... | collective-permute-start | bytes 98312 | tf_op jit(solution)/shard_map/ppermute | solution.py:188

commit v5 on v4

--- a/solution.py
+++ b/solution.py
@@ -68,7 +68,7 @@
     lax.fori_loop(0, (count + UNROLL - 1) // UNROLL, group, 0)
 
 
-def aggregate_kernel(row_turn, turn, meta, x_ref, vals_ref, out_ref, acc):
+def aggregate_kernel(row_turn, col_order, meta, x_ref, vals_ref, out_ref, acc):
     listed, tile = vals_ref.shape[:2]
     per = x_ref.shape[2] // tile
     acc[...] = jnp.zeros_like(acc)
@@ -77,7 +77,7 @@
         at = meta[listed + t]
         start = pl.multiple_of((at % per) * tile, tile)
         return lax.dot_general(
-            x_ref[turned_at(at // per, row_turn, x_ref.shape[0]), :, pl.ds(start, tile)],
+            x_ref[(at // per + x_ref.shape[0] - row_turn) % x_ref.shape[0], :, pl.ds(start, tile)],
             vals_ref[t],
             (((1,), (1,)), ((), ())),
             preferred_element_type=F32,
@@ -87,9 +87,8 @@
         acc[meta[t]] = acc[meta[t]] + found
 
     live_loop(meta[2 * listed], product, add)
-    cut = turn * per
-    out_ref[: acc.shape[0] - cut] = acc[cut:].astype(out_ref.dtype)
-    out_ref[acc.shape[0] - cut :] = acc[:cut].astype(out_ref.dtype)
+    for i, c in enumerate(col_order):
+        out_ref[i * per : (i + 1) * per] = acc[c * per : (c + 1) * per].astype(out_ref.dtype)
 
 
 def tile_kernel(part_ref, w_ref, low_ref, high_ref, out_ref, cot_all):
@@ -113,22 +112,26 @@
     dtype = out_ref.dtype
     out_ref[:, :feat] = dagg.astype(dtype).reshape(groups, feat, tile)
     out_ref[:, feat : feat + outs] = y.astype(dtype).reshape(groups, outs, tile)
-    out_ref[:, feat + outs :] = grad.astype(dtype).reshape(groups, outs, tile)
+    high = grad.astype(dtype)
+    low = (grad - high.astype(F32)).astype(dtype)
+    out_ref[:, feat + outs : feat + 2 * outs] = high.reshape(groups, outs, tile)
+    out_ref[:, feat + 2 * outs :] = low.reshape(groups, outs, tile)
 
 
 def pack_kernel(in_ref, out_ref):
     tiles, in_rows, tile = in_ref.shape
-    outs = (in_rows * tiles - out_ref.shape[1]) // (2 * tiles - 1)
-    feat = in_rows - 2 * outs
+    outs = (in_rows * tiles - out_ref.shape[1]) // (3 * tiles - 1)
+    feat = in_rows - 3 * outs
     rows = tiles * feat
     dagg = in_ref[:, :feat].reshape(rows, tile)
-    grad = jnp.sum(in_ref[:, feat + outs :].astype(F32), axis=0).astype(out_ref.dtype)
+    grad = jnp.sum(in_ref[:, feat + outs :].astype(F32), axis=0)
+    grad = (grad[:outs] + grad[outs:]).astype(out_ref.dtype)
     for i in range(out_ref.shape[0]):
         out_ref[i, :rows] = dagg
         out_ref[i, rows:] = grad
 
 
-def backward_kernel(row_turn, turn, meta, d_ref, vals_ref, out_ref, acc):
+def backward_kernel(row_turn, col_order, meta, d_ref, vals_ref, out_ref, acc):
     listed = vals_ref.shape[0]
     parts, rows, tile = out_ref.shape
     per = acc.shape[0] // parts
@@ -140,7 +143,7 @@
         at = meta[t]
         start = pl.multiple_of((at % per) * feat, feat)
         return jnp.dot(
-            d_ref[turned_at(at // per, turn, d_ref.shape[0]), pl.ds(start, feat), :],
+            d_ref[place_of(at // per, col_order), pl.ds(start, feat), :],
             vals_ref[t],
             preferred_element_type=F32,
         )
@@ -173,13 +176,16 @@
         y_ref[:, i * tile : (i + 1) * tile] = mid_ref[i, feat : feat + outs]
 
 
-def turned_at(member, turn, n):
-    return (member + n - turn) % n
-
-
-def exchange(parts, axis, turn=0):
-    n = lax.axis_size(axis)
-    groups = [[(i + turn) % n for i in range(n)]] if turn else None
+def place_of(member, order):
+    place = jnp.int32(0)
+    for i, listed in enumerate(order):
+        if i > 0:
+            place = jnp.where(member == listed, i, place)
+    return place
+
+
+def exchange(parts, axis, order=None):
+    groups = None if order is None else [list(order)]
     return lax.all_to_all(parts, axis, 0, 0, axis_index_groups=groups, tiled=True)
 
 
@@ -196,13 +202,15 @@
     n_row, n_col, n_rep = lax.axis_size("row"), lax.axis_size("col"), lax.axis_size("rep")
     out_loc = weight.shape[1] // n_rep
     row_turn, col_turn = n_row // 4, n_col // 2
+    row_order = [(i + row_turn) % n_row for i in range(n_row)]
+    col_order = sorted(range(n_col), key=lambda c: (c != col_turn, c != 0, -c))
     grad_shape = (out_loc, n_rep * feat)
     shape = jax.ShapeDtypeStruct
 
     meta = jnp.concatenate([tile_rows[0, 0], tile_cols[0, 0], tile_count[0]])
 
     x_parts = call(copies_kernel, shape((n_row, feat, slab), BF16), [VMEM], "copies")(x_t)
-    x_all = exchange(x_parts, "row", row_turn)
+    x_all = exchange(x_parts, "row", row_order)
     half = shape((n_rep // 2, out_loc, tile), BF16)
     keep, send = call(cut_kernel, (half, half), [VMEM], "cut")(cotangent_t)
     got = swap(send, 1)
@@ -224,15 +232,16 @@
     )(tile_vals[0, 0])
 
     part = call(
-        functools.partial(aggregate_kernel, row_turn, col_turn),
+        functools.partial(aggregate_kernel, row_turn, col_order),
         shape((n_col * per, feat, tile), BF16),
         [SMEM, VMEM, VMEM],
         "aggregate",
         [pltpu.VMEM((n_col * per, feat, tile), F32)],
     )(meta, x_all, vals)
-    part = exchange(part, ("col", "rep"), col_turn * n_rep)
-
-    mid_rows = feat + 2 * out_loc
+    order = [c * n_rep + i for c in col_order for i in range(n_rep)]
+    part = exchange(part, ("col", "rep"), order)
+
+    mid_rows = feat + 3 * out_loc
     mid = call(
         tile_kernel,
         shape((n_rep, mid_rows, tile), BF16),
@@ -242,16 +251,16 @@
     )(part, weight, keep, got)
     mid = exchange(mid, "rep")
     send = call(pack_kernel, shape((n_col, per * feat + out_loc, tile), BF16), [VMEM], "pack")(mid)
-    d_all = exchange(send, "col", col_turn)
+    d_all = exchange(send, "col", col_order)
 
     back = call(
-        functools.partial(backward_kernel, row_turn, col_turn),
+        functools.partial(backward_kernel, row_turn, col_order),
         shape((n_row, per * feat + out_loc, tile), BF16),
         [SMEM, VMEM, VMEM],
         "backward",
         [pltpu.VMEM((n_row * per, feat, tile), F32)],
     )(meta, d_all, vals)
-    back = exchange(back, "row", row_turn)
+    back = exchange(back, "row", row_order)
 
     dx, y, grad = call(
         final_kernel,

time: 107 us -> 108 us (level)
  starting transfers between devices: 41.2 us -> 39.2 us
  blocking collectives: 46.6 us -> 48 us
  Pallas kernels: 7.11 us -> 8.21 us
    all_to_all x2, starting transfers between devices: 30.4 us -> 28.4 us  [exchange(): lax.all_to_all(parts, axis, 0, 0, axis_index_groups=groups, tiled=True)]
    all_to_all x3, blocking collectives: 46.6 us -> 48 us  [exchange(): lax.all_to_all(parts, axis, 0, 0, axis_index_groups=groups, tiled=True)]
    pallas_call x2, Pallas kernels: 3.56 us -> 4.65 us  [the longest x1 3.07 us: local(): call(functools.partial(aggregate_kernel, row_turn, col_order), shape((n_c...]
where the time goes in v5:
time: 108 us; the launch traced here: 107 us
  blocking collectives  48 us (44%)
  starting transfers between devices  39.2 us (36%)
  Pallas kernels  8.21 us (8%)
  waiting for transfers between devices  5.66 us (5%)
  local copies, waits for them, and re-layouts  3.49 us (3%)
  between operations  1.4 us (1%)
    all_to_all x3, blocking collectives, exchange(): lax.all_to_all(parts, axis, 0, 0, axis_index_groups=groups, tiled=True)  48 us
    all_to_all x2, starting transfers between devices, exchange(): lax.all_to_all(parts, axis, 0, 0, axis_index_groups=groups, tiled=True)  28.4 us
    ppermute x3, starting transfers between devices, swap(): return lax.ppermute(parts, 'rep', [(i, i ^ bit) for i in range(n)])  10.9 us
    all_to_all x2, waiting for transfers between devices, exchange(): lax.all_to_all(parts, axis, 0, 0, axis_index_groups=groups, tiled=True)  3.63 us
    unnamed x8, local copies, waits for them, and re-layouts  3.48 us
    pallas_call x1, Pallas kernels, local(): call(functools.partial(aggregate_kernel, row_turn, col_order), shape((n_c...  3.07 us
  transfers between devices with their start and end apart: 5, of which 4 were waited for; matrix products, arithmetic and copies ran while one was open for 1% of the time, Pallas kernels for 1%

profile of v5, /device:TPU:1, one launch (start us, length us, event | category | flops | bytes accessed | tf_op | source)
XLA Modules:
  0.0 106.8 jit_solution(3964881347333721347)
XLA Ops:
  0.6 0.7 copy-done.3
  1.4 0.8 copies.1
  2.2 9.4 %all-to-all-start = ((bf16[16,16,1024]{2,1,0:T(8,128)(2,1)}), bf16[16,16,1024]{2,1,0:T(8,128)(2,1)}, u32[]{:S(2)}, u32[]{:S(2)}) async-start(bf16[16,16,1024]{2,1,0:T(8,128)(2,1)} %copies.1), calls=%async_computation | async-start | bytes 1048576 | tf_op jit(solution)/shard_map/all_to_all | solution.py:189
  11.6 0.8 copy-done.2
  12.5 3.6 %collective-permute-start = (bf16[4,32,128]{2,1,0:T(8,128)(2,1)S(1)}, bf16[4,32,128]{2,1,0:T(8,128)(2,1)S(1)}, u32[]{:S(2)}, u32[]{:S(2)}) collective-permute-start(bf16[4,32,128]{2,1,0:T(8,128)(2,1)S(1)} %get-tuple-element.12), channel_id=1, source_target_pairs={{0,1},{1,0},{2,3},{3,2},{4,5},{5,4},{6,7},{7,6},{8,9},{9,8},{10,11... | collective-permute-start | bytes 98312 | tf_op jit(solution)/shard_map/ppermute | solution.py:194
  16.7 0.2 collective-permute-done
  16.9 2.7 %collective-permute-start.1 = (bf16[4,32,128]{2,1,0:T(8,128)(2,1)S(1)}, bf16[4,32,128]{2,1,0:T(8,128)(2,1)S(1)}, u32[]{:S(2)}, u32[]{:S(2)}) collective-permute-start(bf16[4,32,128]{2,1,0:T(8,128)(2,1)S(1)} %pad_maximum_fusion), channel_id=1, source_target_pairs={{0,2},{1,3},{2,0},{3,1},{4,6},{5,7},{6,4},{7,5},{8,10},{9,11},{10,... | collective-permute-start | bytes 98312 | tf_op jit(solution)/shard_map/ppermute | solution.py:194
  19.6 0.8 pad_add_fusion.meta
  20.4 1.9 %copy-done = bf16[1,1,96,128,128]{4,3,2,1,0:T(8,128)(2,1)S(1)} copy-done((bf16[1,1,96,128,128]{4,3,2,1,0:T(8,128)(2,1)S(1)}, bf16[1,1,96,128,128]{4,3,2,1,0:T(8,128)(2,1)}, u32[]{:S(2)}) %copy-start) | copy-done | bytes 3145752
  22.2 1.6 %stage.1.vals_ref = bf16[96,128,128]{2,1,0:T(8,128)(2,1)S(1)} custom-call(bf16[96,128,128]{2,1,0:T(8,128)(2,1)S(1)} %bitcast.6), custom_call_target="tpu_custom_call" | custom-call | tf_op jit(solution)/shard_map/stage/pallas_call | solution.py:226
  23.8 0.0 copy-start.1
  23.8 0.0 collective-permute-done.1
  23.9 0.5 all-to-all-done.x_ref
  24.4 3.1 %aggregate.1 = bf16[32,16,128]{2,1,0:T(8,128)(2,1)} custom-call(s32[193]{0:T(256)S(1)} %pad_add_fusion.meta, bf16[16,16,1024]{2,1,0:T(8,128)(2,1)} %all-to-all-done.x_ref, bf16[96,128,128]{2,1,0:T(8,128)(2,1)S(1)} %stage.1.vals_ref), custom_call_target="tpu_custom_call" | custom-call | tf_op jit(solution)/shard_map/aggregate/pallas_call | solution.py:234
  27.5 19.0 %all-to-all-start.1 = ((bf16[32,16,128]{2,1,0:T(8,128)(2,1)}), bf16[32,16,128]{2,1,0:T(8,128)(2,1)S(1)}, u32[]{:S(2)}, u32[]{:S(2)}) async-start(bf16[32,16,128]{2,1,0:T(8,128)(2,1)} %aggregate.1), calls=%async_computation.1 | async-start | bytes 262144 | tf_op jit(solution)/shard_map/all_to_all | solution.py:189
  46.5 4.6 %collective-permute-start.2 = (bf16[4,32,128]{2,1,0:T(8,128)(2,1)S(1)}, bf16[4,32,128]{2,1,0:T(8,128)(2,1)S(1)}, u32[]{:S(2)}, u32[]{:S(2)}) collective-permute-start(bf16[4,32,128]{2,1,0:T(8,128)(2,1)S(1)} %get-tuple-element.15), channel_id=1, source_target_pairs={{0,4},{1,5},{2,6},{3,7},{4,0},{5,1},{6,2},{7,3},{8,12},{9,13},{10,... | collective-permute-start | bytes 98312 | tf_op jit(solution)/shard_map/ppermute | solution.py:194
  51.1 1.9 %collective-permute-done.2.high_ref = bf16[4,32,128]{2,1,0:T(8,128)(2,1)S(1)} collective-permute-done((bf16[4,32,128]{2,1,0:T(8,128)(2,1)S(1)}, bf16[4,32,128]{2,1,0:T(8,128)(2,1)S(1)}, u32[]{:S(2)}, u32[]{:S(2)}) %collective-permute-start.2) | collective-permute-done | bytes 32800 | tf_op jit(solution)/shard_map/ppermute | solution.py:194
  52.9 3.1 %all-to-all-done.1.part_ref = bf16[32,16,128]{2,1,0:T(8,128)(2,1)S(1)} async-done(((bf16[32,16,128]{2,1,0:T(8,128)(2,1)}), bf16[32,16,128]{2,1,0:T(8,128)(2,1)S(1)}, u32[]{:S(2)}, u32[]{:S(2)}) %all-to-all-start.1) | async-done | bytes 131104 | tf_op jit(solution)/shard_map/all_to_all | solution.py:189
  56.0 0.4 tile.1
  56.4 8.6 %all_to_all.25.in_ref.mid_ref = bf16[8,112,128]{2,1,0:T(8,128)(2,1)S(1)} all-to-all(bf16[8,112,128]{2,1,0:T(8,128)(2,1)S(1)} %tile.1), channel_id=1, replica_groups=mesh['row'=16,'col'=4,'rep'=8] {'rep'}, dimensions={0} | all-to-all | bytes 458752 | tf_op jit(solution)/shard_map/all_to_all | solution.py:189
  65.0 17.6 %all_to_all.26.d_ref = bf16[4,160,128]{2,1,0:T(8,128)(2,1)S(1)} all-to-all(bf16[4,160,128]{2,1,0:T(8,128)(2,1)S(1)} %pack.1), channel_id=1, replica_groups={{16,0,24,8},{17,1,25,9},{18,2,26,10},{19,3,27,11},{20,4,28,12},{21,5,29..., dimensions={0} | all-to-all | bytes 327680 | tf_op jit(solution)/shard_map/all_to_all | solution.py:189
  82.6 1.6 %backward.1 = bf16[16,160,128]{2,1,0:T(8,128)(2,1)S(1)} custom-call(s32[193]{0:T(256)S(1)} %pad_add_fusion.meta, bf16[4,160,128]{2,1,0:T(8,128)(2,1)S(1)} %all_to_all.26.d_ref, bf16[96,128,128]{2,1,0:T(8,128)(2,1)S(1)} %stage.1.vals_ref), custom_call_target="tpu_custom_call" | custom-call | tf_op jit(solution)/shard_map/backward/pallas_call | solution.py:256
  84.2 21.9 %all_to_all.27.in_ref = bf16[16,160,128]{2,1,0:T(8,128)(2,1)S(1)} all-to-all(bf16[16,160,128]{2,1,0:T(8,128)(2,1)S(1)} %backward.1), channel_id=1, replica_groups={{128,160,192,224,256,288,320,352,384,416,448,480,0,32,64,96},{129,161,1..., dimensions={0} | all-to-all | bytes 1310720 | tf_op jit(solution)/shard_map/all_to_all | solution.py:189
  106.1 0.7 final.1
  (11 shorter events, 0.1 us)
Async XLA Ops:
  0.6 0.8 copy-start.3
  2.2 22.2 %all-to-all-start = ((bf16[16,16,1024]{2,1,0:T(8,128)(2,1)}), bf16[16,16,1024]{2,1,0:T(8,128)(2,1)}, u32[]{:S(2)}, u32[]{:S(2)}) async-start(bf16[16,16,1024]{2,1,0:T(8,128)(2,1)} %copies.1), calls=%async_computation | async-start | bytes 1048576 | tf_op jit(solution)/shard_map/all_to_all | solution.py:189
  11.6 0.8 copy-start.2
  12.5 4.4 %collective-permute-start = (bf16[4,32,128]{2,1,0:T(8,128)(2,1)S(1)}, bf16[4,32,128]{2,1,0:T(8,128)(2,1)S(1)}, u32[]{:S(2)}, u32[]{:S(2)}) collective-permute-start(bf16[4,32,128]{2,1,0:T(8,128)(2,1)S(1)} %get-tuple-element.12), channel_id=1, source_target_pairs={{0,1},{1,0},{2,3},{3,2},{4,5},{5,4},{6,7},{7,6},{8,9},{9,8},{10,11... | collective-permute-start | bytes 98312 | tf_op jit(solution)/shard_map/ppermute | solution.py:194
  16.9 7.0 %collective-permute-start.1 = (bf16[4,32,128]{2,1,0:T(8,128)(2,1)S(1)}, bf16[4,32,128]{2,1,0:T(8,128)(2,1)S(1)}, u32[]{:S(2)}, u32[]{:S(2)}) collective-permute-start(bf16[4,32,128]{2,1,0:T(8,128)(2,1)S(1)} %pad_maximum_fusion), channel_id=1, source_target_pairs={{0,2},{1,3},{2,0},{3,1},{4,6},{5,7},{6,4},{7,5},{8,10},{9,11},{10,... | collective-permute-start | bytes 98312 | tf_op jit(solution)/shard_map/ppermute | solution.py:194
  20.3 1.9 %copy-start = (bf16[1,1,96,128,128]{4,3,2,1,0:T(8,128)(2,1)S(1)}, bf16[1,1,96,128,128]{4,3,2,1,0:T(8,128)(2,1)}, u32[]{:S(2)}) copy-start(bf16[1,1,96,128,128]{4,3,2,1,0:T(8,128)(2,1)} %param.10) | copy-start | bytes 9437188
  23.8 32.2 %copy-start.1 = (bf16[128,256]{1,0:T(8,128)(2,1)S(1)}, bf16[128,256]{1,0:T(8,128)(2,1)}, u32[]{:S(2)}) copy-start(bf16[128,256]{1,0:T(8,128)(2,1)} %w_ref.1) | copy-start | bytes 196612
  27.5 28.6 %all-to-all-start.1 = ((bf16[32,16,128]{2,1,0:T(8,128)(2,1)}), bf16[32,16,128]{2,1,0:T(8,128)(2,1)S(1)}, u32[]{:S(2)}, u32[]{:S(2)}) async-start(bf16[32,16,128]{2,1,0:T(8,128)(2,1)} %aggregate.1), calls=%async_computation.1 | async-start | bytes 262144 | tf_op jit(solution)/shard_map/all_to_all | solution.py:189
  46.5 6.5 %collective-permute-start.2 = (bf16[4,32,128]{2,1,0:T(8,128)(2,1)S(1)}, bf16[4,32,128]{2,1,0:T(8,128)(2,1)S(1)}, u32[]{:S(2)}, u32[]{:S(2)}) collective-permute-start(bf16[4,32,128]{2,1,0:T(8,128)(2,1)S(1)} %get-tuple-element.15), channel_id=1, source_target_pairs={{0,4},{1,5},{2,6},{3,7},{4,0},{5,1},{6,2},{7,3},{8,12},{9,13},{10,... | collective-permute-start | bytes 98312 | tf_op jit(solution)/shard_map/ppermute | solution.py:194

commit v6 on v5

--- a/solution.py
+++ b/solution.py
@@ -131,12 +131,13 @@
         out_ref[i, rows:] = grad
 
 
-def backward_kernel(row_turn, col_order, meta, d_ref, vals_ref, out_ref, acc):
+def backward_kernel(grad_rows, col_order, meta, d_ref, vals_ref, out_ref, acc):
     listed = vals_ref.shape[0]
-    parts, rows, tile = out_ref.shape
-    per = acc.shape[0] // parts
+    inner, rows, tile = out_ref.shape
     feat = acc.shape[1]
-    slab_rows = per * feat
+    slab_rows = d_ref.shape[1] - grad_rows
+    per = slab_rows // feat
+    outer = rows // slab_rows
     acc[...] = jnp.zeros_like(acc)
 
     def product(t):
@@ -154,12 +155,23 @@
 
     live_loop(meta[2 * listed], product, add)
     grad = jnp.sum(d_ref[:, slab_rows:, :].astype(F32), axis=0).astype(out_ref.dtype)
-    for i in range(parts):
-        r = (i + row_turn) % parts
-        out_ref[i, :slab_rows] = (
-            acc[r * per : (r + 1) * per].reshape(slab_rows, tile).astype(out_ref.dtype)
-        )
-        out_ref[i, slab_rows:] = grad
+    for i in range(inner):
+        for o in range(outer):
+            first = (o * inner + i) * per
+            out_ref[i, o * slab_rows : (o + 1) * slab_rows] = (
+                acc[first : first + per].reshape(slab_rows, tile).astype(out_ref.dtype)
+            )
+        out_ref[i, outer * slab_rows :] = grad
+
+
+def fold_kernel(turn, in_ref, out_ref):
+    outer, rows, _ = out_ref.shape
+    total = jnp.sum(in_ref[...].astype(F32), axis=0).astype(out_ref.dtype)
+    slab_rows = (total.shape[0] - rows) // (outer - 1)
+    for i in range(outer):
+        o = (i + turn) % outer
+        out_ref[i, :slab_rows] = total[o * slab_rows : (o + 1) * slab_rows]
+        out_ref[i, slab_rows:] = total[outer * slab_rows :]
 
 
 def final_kernel(in_ref, mid_ref, dx_ref, y_ref, grad_ref):
@@ -204,6 +216,13 @@
     row_turn, col_turn = n_row // 4, n_col // 2
     row_order = [(i + row_turn) % n_row for i in range(n_row)]
     col_order = sorted(range(n_col), key=lambda c: (c != col_turn, c != 0, -c))
+    inner = 4 if n_row % 4 == 0 else 1
+    outer = n_row // inner
+    outer_turn = outer // 4
+    inner_groups = [[o * inner + i for i in range(inner)] for o in range(outer)]
+    outer_groups = [
+        [(o + outer_turn) % outer * inner + i for o in range(outer)] for i in range(inner)
+    ]
     grad_shape = (out_loc, n_rep * feat)
     shape = jax.ShapeDtypeStruct
 
@@ -254,13 +273,20 @@
     d_all = exchange(send, "col", col_order)
 
     back = call(
-        functools.partial(backward_kernel, row_turn, col_order),
-        shape((n_row, per * feat + out_loc, tile), BF16),
+        functools.partial(backward_kernel, out_loc, col_order),
+        shape((inner, outer * per * feat + out_loc, tile), BF16),
         [SMEM, VMEM, VMEM],
         "backward",
         [pltpu.VMEM((n_row * per, feat, tile), F32)],
     )(meta, d_all, vals)
-    back = exchange(back, "row", row_order)
+    back = lax.all_to_all(back, "row", 0, 0, axis_index_groups=inner_groups, tiled=True)
+    back = call(
+        functools.partial(fold_kernel, outer_turn),
+        shape((outer, per * feat + out_loc, tile), BF16),
+        [VMEM],
+        "fold",
+    )(back)
+    back = lax.all_to_all(back, "row", 0, 0, axis_index_groups=outer_groups, tiled=True)
 
     dx, y, grad = call(
         final_kernel,

time: 108 us -> 107 us (level)
  blocking collectives: 48 us -> 46.9 us
  Pallas kernels: 8.21 us -> 7.12 us
    all_to_all x3 -> x2, blocking collectives: 48 us -> 26.1 us  [exchange(): lax.all_to_all(parts, axis, 0, 0, axis_index_groups=groups, tiled=True)]
    all_to_all x0 -> x2, blocking collectives: none -> 20.8 us  [the longest x1 11.3 us: local(): lax.all_to_all(back, 'row', 0, 0, axis_index_groups=outer_groups, tiled=T...]
  transfers between devices with their start and end apart: 5 -> 5, of which waited for: 4 -> 4; matrix products, arithmetic and copies ran while one was open for 1% -> 1% of each run, Pallas kernels for 1% -> 2%
where the time goes in v6:
time: 107 us; the launch traced here: 105 us
  blocking collectives  46.9 us (44%)
  starting transfers between devices  39.9 us (37%)
  Pallas kernels  7.12 us (7%)
  waiting for transfers between devices  5.66 us (5%)
  local copies, waits for them, and re-layouts  3.49 us (3%)
  between operations  1.4 us (1%)
    all_to_all x2, starting transfers between devices, exchange(): lax.all_to_all(parts, axis, 0, 0, axis_index_groups=groups, tiled=True)  29 us
    all_to_all x2, blocking collectives, exchange(): lax.all_to_all(parts, axis, 0, 0, axis_index_groups=groups, tiled=True)  26.1 us
    all_to_all x1, blocking collectives, local(): lax.all_to_all(back, 'row', 0, 0, axis_index_groups=outer_groups, tiled=T...  11.3 us
    ppermute x3, starting transfers between devices, swap(): return lax.ppermute(parts, 'rep', [(i, i ^ bit) for i in range(n)])  10.9 us
    all_to_all x1, blocking collectives, local(): lax.all_to_all(back, 'row', 0, 0, axis_index_groups=inner_groups, tiled=T...  9.48 us
    all_to_all x2, waiting for transfers between devices, exchange(): lax.all_to_all(parts, axis, 0, 0, axis_index_groups=groups, tiled=True)  3.63 us
    unnamed x8, local copies, waits for them, and re-layouts  3.48 us
    pallas_call x1, Pallas kernels, local(): call(functools.partial(aggregate_kernel, row_turn, col_order), shape((n_c...  2.41 us
  transfers between devices with their start and end apart: 5, of which 4 were waited for; matrix products, arithmetic and copies ran while one was open for 1% of the time, Pallas kernels for 2%

profile of v6, /device:TPU:1, one launch (start us, length us, event | category | flops | bytes accessed | tf_op | source)
XLA Modules:
  0.0 105.3 jit_solution(5861182332844366077)
XLA Ops:
  0.6 0.7 copy-done.3
  1.4 0.8 copies.1
  2.2 9.4 %all-to-all-start = ((bf16[16,16,1024]{2,1,0:T(8,128)(2,1)}), bf16[16,16,1024]{2,1,0:T(8,128)(2,1)}, u32[]{:S(2)}, u32[]{:S(2)}) async-start(bf16[16,16,1024]{2,1,0:T(8,128)(2,1)} %copies.1), calls=%async_computation | async-start | bytes 1048576 | tf_op jit(solution)/shard_map/all_to_all | solution.py:201
  11.6 0.8 copy-done.2
  12.5 3.6 %collective-permute-start = (bf16[4,32,128]{2,1,0:T(8,128)(2,1)S(1)}, bf16[4,32,128]{2,1,0:T(8,128)(2,1)S(1)}, u32[]{:S(2)}, u32[]{:S(2)}) collective-permute-start(bf16[4,32,128]{2,1,0:T(8,128)(2,1)S(1)} %get-tuple-element.12), channel_id=1, source_target_pairs={{0,1},{1,0},{2,3},{3,2},{4,5},{5,4},{6,7},{7,6},{8,9},{9,8},{10,11... | collective-permute-start | bytes 98312 | tf_op jit(solution)/shard_map/ppermute | solution.py:206
  16.7 0.2 collective-permute-done
  16.9 2.7 %collective-permute-start.1 = (bf16[4,32,128]{2,1,0:T(8,128)(2,1)S(1)}, bf16[4,32,128]{2,1,0:T(8,128)(2,1)S(1)}, u32[]{:S(2)}, u32[]{:S(2)}) collective-permute-start(bf16[4,32,128]{2,1,0:T(8,128)(2,1)S(1)} %pad_maximum_fusion), channel_id=1, source_target_pairs={{0,2},{1,3},{2,0},{3,1},{4,6},{5,7},{6,4},{7,5},{8,10},{9,11},{10,... | collective-permute-start | bytes 98312 | tf_op jit(solution)/shard_map/ppermute | solution.py:206
  19.6 0.8 pad_add_fusion.meta
  20.4 1.9 %copy-done = bf16[1,1,96,128,128]{4,3,2,1,0:T(8,128)(2,1)S(1)} copy-done((bf16[1,1,96,128,128]{4,3,2,1,0:T(8,128)(2,1)S(1)}, bf16[1,1,96,128,128]{4,3,2,1,0:T(8,128)(2,1)}, u32[]{:S(2)}) %copy-start) | copy-done | bytes 3145752
  22.2 1.6 %stage.1.vals_ref = bf16[96,128,128]{2,1,0:T(8,128)(2,1)S(1)} custom-call(bf16[96,128,128]{2,1,0:T(8,128)(2,1)S(1)} %bitcast.6), custom_call_target="tpu_custom_call" | custom-call | tf_op jit(solution)/shard_map/stage/pallas_call | solution.py:245
  23.9 0.5 all-to-all-done.x_ref
  24.4 2.4 %aggregate.1 = bf16[32,16,128]{2,1,0:T(8,128)(2,1)} custom-call(s32[193]{0:T(256)S(1)} %pad_add_fusion.meta, bf16[16,16,1024]{2,1,0:T(8,128)(2,1)} %all-to-all-done.x_ref, bf16[96,128,128]{2,1,0:T(8,128)(2,1)S(1)} %stage.1.vals_ref), custom_call_target="tpu_custom_call" | custom-call | tf_op jit(solution)/shard_map/aggregate/pallas_call | solution.py:253
  26.8 19.7 %all-to-all-start.1 = ((bf16[32,16,128]{2,1,0:T(8,128)(2,1)}), bf16[32,16,128]{2,1,0:T(8,128)(2,1)S(1)}, u32[]{:S(2)}, u32[]{:S(2)}) async-start(bf16[32,16,128]{2,1,0:T(8,128)(2,1)} %aggregate.1), calls=%async_computation.1 | async-start | bytes 262144 | tf_op jit(solution)/shard_map/all_to_all | solution.py:201
  46.5 4.6 %collective-permute-start.2 = (bf16[4,32,128]{2,1,0:T(8,128)(2,1)S(1)}, bf16[4,32,128]{2,1,0:T(8,128)(2,1)S(1)}, u32[]{:S(2)}, u32[]{:S(2)}) collective-permute-start(bf16[4,32,128]{2,1,0:T(8,128)(2,1)S(1)} %get-tuple-element.15), channel_id=1, source_target_pairs={{0,4},{1,5},{2,6},{3,7},{4,0},{5,1},{6,2},{7,3},{8,12},{9,13},{10,... | collective-permute-start | bytes 98312 | tf_op jit(solution)/shard_map/ppermute | solution.py:206
  51.1 1.9 %collective-permute-done.2.high_ref = bf16[4,32,128]{2,1,0:T(8,128)(2,1)S(1)} collective-permute-done((bf16[4,32,128]{2,1,0:T(8,128)(2,1)S(1)}, bf16[4,32,128]{2,1,0:T(8,128)(2,1)S(1)}, u32[]{:S(2)}, u32[]{:S(2)}) %collective-permute-start.2) | collective-permute-done | bytes 32800 | tf_op jit(solution)/shard_map/ppermute | solution.py:206
  52.9 3.1 %all-to-all-done.1.part_ref = bf16[32,16,128]{2,1,0:T(8,128)(2,1)S(1)} async-done(((bf16[32,16,128]{2,1,0:T(8,128)(2,1)}), bf16[32,16,128]{2,1,0:T(8,128)(2,1)S(1)}, u32[]{:S(2)}, u32[]{:S(2)}) %all-to-all-start.1) | async-done | bytes 131104 | tf_op jit(solution)/shard_map/all_to_all | solution.py:201
  56.0 0.4 tile.1
  56.4 8.6 %all_to_all.30.in_ref.mid_ref = bf16[8,112,128]{2,1,0:T(8,128)(2,1)S(1)} all-to-all(bf16[8,112,128]{2,1,0:T(8,128)(2,1)S(1)} %tile.1), channel_id=1, replica_groups=mesh['row'=16,'col'=4,'rep'=8] {'rep'}, dimensions={0} | all-to-all | bytes 458752 | tf_op jit(solution)/shard_map/all_to_all | solution.py:201
  65.0 17.6 %all_to_all.31.d_ref = bf16[4,160,128]{2,1,0:T(8,128)(2,1)S(1)} all-to-all(bf16[4,160,128]{2,1,0:T(8,128)(2,1)S(1)} %pack.1), channel_id=1, replica_groups={{16,0,24,8},{17,1,25,9},{18,2,26,10},{19,3,27,11},{20,4,28,12},{21,5,29..., dimensions={0} | all-to-all | bytes 327680 | tf_op jit(solution)/shard_map/all_to_all | solution.py:201
  82.6 1.1 %backward.1 = bf16[4,544,128]{2,1,0:T(8,128)(2,1)S(1)} custom-call(s32[193]{0:T(256)S(1)} %pad_add_fusion.meta, bf16[4,160,128]{2,1,0:T(8,128)(2,1)S(1)} %all_to_all.31.d_ref, bf16[96,128,128]{2,1,0:T(8,128)(2,1)S(1)} %stage.1.vals_ref), custom_call_target="tpu_custom_call" | custom-call | tf_op jit(solution)/shard_map/backward/pallas_call | solution.py:275
  83.8 9.5 %all_to_all.32.in_ref = bf16[4,544,128]{2,1,0:T(8,128)(2,1)S(1)} all-to-all(bf16[4,544,128]{2,1,0:T(8,128)(2,1)S(1)} %backward.1), channel_id=1, replica_groups={{0,32,64,96},{128,160,192,224},{256,288,320,352},{384,416,448,480},{1,3..., dimensions={0} | all-to-all | bytes 1114112 | tf_op jit(solution)/shard_map/all_to_all | solution.py:282
  93.2 0.1 fold.1
  93.3 11.3 %all_to_all.33.in_ref = bf16[4,160,128]{2,1,0:T(8,128)(2,1)S(1)} all-to-all(bf16[4,160,128]{2,1,0:T(8,128)(2,1)S(1)} %fold.1), channel_id=1, replica_groups={{128,256,384,0},{160,288,416,32},{192,320,448,64},{224,352,480,96},{129..., dimensions={0} | all-to-all | bytes 327680 | tf_op jit(solution)/shard_map/all_to_all | solution.py:289
  104.6 0.7 final.1
  (13 shorter events, 0.1 us)
Async XLA Ops:
  0.6 0.8 copy-start.3
  2.2 22.2 %all-to-all-start = ((bf16[16,16,1024]{2,1,0:T(8,128)(2,1)}), bf16[16,16,1024]{2,1,0:T(8,128)(2,1)}, u32[]{:S(2)}, u32[]{:S(2)}) async-start(bf16[16,16,1024]{2,1,0:T(8,128)(2,1)} %copies.1), calls=%async_computation | async-start | bytes 1048576 | tf_op jit(solution)/shard_map/all_to_all | solution.py:201
  11.6 0.8 copy-start.2
  12.5 4.4 %collective-permute-start = (bf16[4,32,128]{2,1,0:T(8,128)(2,1)S(1)}, bf16[4,32,128]{2,1,0:T(8,128)(2,1)S(1)}, u32[]{:S(2)}, u32[]{:S(2)}) collective-permute-start(bf16[4,32,128]{2,1,0:T(8,128)(2,1)S(1)} %get-tuple-element.12), channel_id=1, source_target_pairs={{0,1},{1,0},{2,3},{3,2},{4,5},{5,4},{6,7},{7,6},{8,9},{9,8},{10,11... | collective-permute-start | bytes 98312 | tf_op jit(solution)/shard_map/ppermute | solution.py:206
  16.9 7.0 %collective-permute-start.1 = (bf16[4,32,128]{2,1,0:T(8,128)(2,1)S(1)}, bf16[4,32,128]{2,1,0:T(8,128)(2,1)S(1)}, u32[]{:S(2)}, u32[]{:S(2)}) collective-permute-start(bf16[4,32,128]{2,1,0:T(8,128)(2,1)S(1)} %pad_maximum_fusion), channel_id=1, source_target_pairs={{0,2},{1,3},{2,0},{3,1},{4,6},{5,7},{6,4},{7,5},{8,10},{9,11},{10,... | collective-permute-start | bytes 98312 | tf_op jit(solution)/shard_map/ppermute | solution.py:206
  20.3 1.9 %copy-start = (bf16[1,1,96,128,128]{4,3,2,1,0:T(8,128)(2,1)S(1)}, bf16[1,1,96,128,128]{4,3,2,1,0:T(8,128)(2,1)}, u32[]{:S(2)}) copy-start(bf16[1,1,96,128,128]{4,3,2,1,0:T(8,128)(2,1)} %param.10) | copy-start | bytes 9437188
  23.8 32.2 %copy-start.1 = (bf16[128,256]{1,0:T(8,128)(2,1)S(1)}, bf16[128,256]{1,0:T(8,128)(2,1)}, u32[]{:S(2)}) copy-start(bf16[128,256]{1,0:T(8,128)(2,1)} %w_ref.1) | copy-start | bytes 196612
  26.8 29.2 %all-to-all-start.1 = ((bf16[32,16,128]{2,1,0:T(8,128)(2,1)}), bf16[32,16,128]{2,1,0:T(8,128)(2,1)S(1)}, u32[]{:S(2)}, u32[]{:S(2)}) async-start(bf16[32,16,128]{2,1,0:T(8,128)(2,1)} %aggregate.1), calls=%async_computation.1 | async-start | bytes 262144 | tf_op jit(solution)/shard_map/all_to_all | solution.py:201
  46.5 6.5 %collective-permute-start.2 = (bf16[4,32,128]{2,1,0:T(8,128)(2,1)S(1)}, bf16[4,32,128]{2,1,0:T(8,128)(2,1)S(1)}, u32[]{:S(2)}, u32[]{:S(2)}) collective-permute-start(bf16[4,32,128]{2,1,0:T(8,128)(2,1)S(1)} %get-tuple-element.15), channel_id=1, source_target_pairs={{0,4},{1,5},{2,6},{3,7},{4,0},{5,1},{6,2},{7,3},{8,12},{9,13},{10,... | collective-permute-start | bytes 98312 | tf_op jit(solution)/shard_map/ppermute | solution.py:206
